TPU v7x, 32 devices: a whole 2x2x4 slice. The times are simulated.
32 devices in a mesh: gz: 4 (over x, core), xy: 8 (over z, y).
Axes of the slice: x: 2, y: 2, z: 4, core: 2. Of those that a mesh axis runs over, the one named last changes fastest.
Arguments:
- volume: bfloat16 [128, 64, 20480], P('gz', None, 'xy'), may hold values from -6 to 6
- occupancy: int32 [4, 160], P('gz', 'xy'), may hold values from 0 to 1, as said below
- device_order: int32 [4, 8], P('gz'), may hold values from 0 to 7, each once within a row
- weight_one: bfloat16 [64, 576], replicated, may hold values from -0.25 to 0.25
- bias_one: float32 [64], replicated, may hold values from -3 to 3
- weight_two: bfloat16 [64, 1728], replicated, may hold values from -0.15625 to 0.15625
- bias_two: float32 [64], replicated, may hold values from -3 to 3
Outputs:
- features: bfloat16 [320, 64, 512], P(('gz', 'xy'))
Inputs may be any that keep to these rules, and one draw needn't show every extreme that they name: `occupancy`: each slab holds exactly 80 tissue bricks, and in each slab all 20 bricks of one xy index are tissue. `device_order`: each slab's row names every xy index once.
All inputs are finite; a program needn't handle non-finite values.
Results may differ from a plain program's by a relative error of at most 0.0025.
Values may be sent and summed in bfloat16 or wider, within the bound.
A program may use at most 256 MiB of HBM per device.

v0:
```python
import jax
import jax.numpy as jnp
from jax import lax
from jax.sharding import PartitionSpec as P


def padded(value, sides, width):
    for axis, dim in sides:
        peers, length = (lax.axis_size(axis), value.shape[dim])
        up = [(i, (i + 1) % peers) for i in range(peers - 1)]
        down = [(j, i) for i, j in up]
        last = lax.slice_in_dim(value, length - width, length, axis=dim)
        leading = lax.slice_in_dim(value, 0, width, axis=dim)
        before = lax.ppermute(last, axis, up)
        after = lax.ppermute(leading, axis, down)
        value = jnp.concatenate([before, value, after], axis=dim)
    return value


def zone_table(length):
    position = jnp.arange(length)
    lower_end = (position == 0).astype(jnp.float32)
    upper_end = (position == length - 1).astype(jnp.float32)
    middle = 1.0 - lower_end - upper_end
    return jnp.stack([lower_end, middle, upper_end], axis=1)


def conv_chain(extended, flags, weight_one, bias_one, weight_two, bias_two):
    count, layers, channels, rows_ext, across = extended.shape
    inner_size = layers - 2
    kernel_one = weight_one.reshape(channels, 1, 3, 3, channels)
    first_sum = lax.conv_general_dilated(
        extended,
        kernel_one,
        (1, 1, 1),
        ((0, 0), (0, 0), (1, 1)),
        dimension_numbers=("NDCHW", "ODHWI", "NCDHW"),
        preferred_element_type=jnp.float32,
    )
    first_act = jax.nn.relu(first_sum + bias_one[None, :, None, None, None])
    region = jnp.einsum(
        "za,nab,yb->nzy", zone_table(layers), flags.astype(jnp.float32), zone_table(inner_size + 2)
    )
    hidden = (first_act * region[:, None, :, :, None]).astype(jnp.bfloat16)
    kernel_two = weight_two.reshape(channels, 3, 3, 3, channels)
    second_sum = lax.conv_general_dilated(
        hidden,
        kernel_two,
        (1, 1, 1),
        ((0, 0), (0, 0), (1, 1)),
        dimension_numbers=("NCDHW", "ODHWI", "NCDHW"),
        preferred_element_type=jnp.float32,
    )
    second_act = jax.nn.relu(second_sum + bias_two[None, :, None, None, None])
    second_act = second_act.reshape(
        count, channels, inner_size // 2, 2, inner_size // 2, 2, across // 2, 2
    )
    pooled = jnp.mean(second_act, axis=(3, 5, 7))
    return pooled.reshape(count, channels, -1).astype(jnp.bfloat16)


def per_device(volume, occupancy, device_order, weight_one, bias_one, weight_two, bias_two):
    brick_side, channels, span = volume.shape
    columns = occupancy.shape[1]
    across = span // (columns * brick_side)
    groups = lax.axis_size("xy")
    capacity = (columns + groups - 1) // groups
    slot_count = columns // 2
    brick_span = brick_side * across
    tissue_row = occupancy[0]
    indicator = jnp.repeat(tissue_row.astype(jnp.bfloat16), brick_span)
    masked = volume * indicator[None, None, :]
    tissue_halo = padded(occupancy, (("gz", 0), ("xy", 1)), 1)
    z_extended = padded(masked, (("gz", 0),), 1)
    full_rims = padded(z_extended, (("xy", 2),), 2 * across)
    own_count = jnp.sum(tissue_row).reshape(1)
    all_counts = lax.all_gather(own_count, "xy", axis=0, tiled=True)
    own_index = lax.axis_index("xy")
    label_ids = jnp.arange(groups, dtype=jnp.int32)
    starts = jnp.cumsum(all_counts) - all_counts
    own_start = jnp.sum(jnp.where(label_ids == own_index, starts, 0))
    local_rank = jnp.cumsum(tissue_row) - tissue_row
    global_index = own_start + local_rank
    label_of = global_index % groups
    order_row = device_order[0]
    destination = jnp.sum(
        jnp.where(label_of[:, None] == label_ids[None, :], order_row[None, :], 0), axis=1
    )
    slot_out = destination * capacity + local_rank // groups
    buffer_ids = jnp.arange(groups * capacity, dtype=jnp.int32)
    matches = (slot_out[None, :] == buffer_ids[:, None]) & (tissue_row[None, :] > 0)
    source_column = jnp.sum(
        jnp.where(matches, jnp.arange(columns, dtype=jnp.int32)[None, :], 0), axis=1
    )
    own_label = jnp.sum(jnp.where(order_row == own_index, label_ids, 0))
    wanted_index = jnp.arange(slot_count, dtype=jnp.int32) * groups + own_label
    range_ends = starts + all_counts
    anchor_device = jnp.sum(
        (range_ends[None, :] <= wanted_index[:, None]).astype(jnp.int32), axis=1
    )
    anchor_start = jnp.sum(
        jnp.where(label_ids[None, :] == anchor_device[:, None], starts[None, :], 0), axis=1
    )
    arrival = anchor_device * capacity + (wanted_index - anchor_start) // groups

    def cut_brick(column_index):
        return lax.dynamic_slice_in_dim(
            full_rims, column_index * brick_span, (brick_side + 4) * across, 2
        )

    def cut_flags(column_index):
        return lax.dynamic_slice(tissue_halo, (jnp.int32(0), column_index), (3, 3)).astype(
            jnp.bfloat16
        )

    picked = jax.vmap(cut_brick)(source_column)
    picked_flags = jax.vmap(cut_flags)(source_column)
    arrived, arrived_flags = (
        lax.all_to_all(picked, "xy", split_axis=0, concat_axis=0, tiled=True),
        lax.all_to_all(picked_flags, "xy", split_axis=0, concat_axis=0, tiled=True),
    )
    chosen_bricks = jnp.take(arrived, arrival, axis=0)
    chosen_flags = jnp.take(arrived_flags, arrival, axis=0)
    shaped = chosen_bricks.reshape(
        chosen_bricks.shape[0], brick_side + 2, channels, brick_side + 4, across
    )
    return conv_chain(shaped, chosen_flags, weight_one, bias_one, weight_two, bias_two)


def solution(mesh):
    in_specs = (P("gz", None, "xy"), P("gz", "xy"), P("gz", None), P(), P(), P(), P())
    out_specs = P(("gz", "xy"), None, None)
    return jax.shard_map(
        per_device, mesh=mesh, in_specs=in_specs, out_specs=out_specs, check_vma=False
    )
```

profile of v0, /device:TPU:0, one launch (start us, length us, event | category | flops | bytes accessed | tf_op | source)
XLA Modules:
  0.0 1036.4 jit_solution(18296606350258400726)
XLA Ops:
  0.0 2.5 collective-permute-start.4
  2.5 1.3 collective-permute-start.5
  3.8 1.4 reduce_sum.76
  5.2 1.2 dynamic-slice.4
  6.4 1.4 dynamic-update-slice.2
  7.8 12.4 %all-reduce.2 = s32[8]{0:T(128)S(1)} all-reduce(s32[8]{0:T(128)S(1)} %dynamic-update-slice.2), channel_id=1, replica_groups=mesh['gz'=4,'xy'=8] {'xy'}, use_global_device_ids=true, to_apply=%add.2 | all-reduce | flops 8 | bytes 64
  20.4 0.7 copy.81
  21.3 0.7 fusion.13
  22.0 1.4 and_select_fusion.2
  23.4 0.7 select_reduce_fusion.1
  24.1 0.7 fusion.19
  24.8 5.5 broadcast_multiply_fusion
  30.3 4.0 copy-done.1
  34.4 1.4 collective-permute-start
  35.8 1.3 collective-permute-start.1
  37.4 3.4 collective-permute-start.6
  40.8 1.3 collective-permute-start.7
  42.1 4.2 collective-permute-done.7
  46.4 5.9 pad_maximum_fusion.1
  52.2 4.1 copy-done
  57.1 1.3 collective-permute-start.3
  58.4 4.5 collective-permute-start.2
  62.9 34.5 %while.1 = (s32[]{:T(128)}, s32[3,22]{1,0:T(4,128)S(1)}, s32[24,2]{0,1:T(2,128)S(1)}, s32[24,3,3]{2,1,0:T(4,128)S(1)}, s32[]{:T(128)}) while((s32[]{:T(128)}, s32[3,22]{1,0:T(4,128)S(1)}, s32[24,2]{0,1:T(2,128)S(1)}, s32[24,3,3]{2,1,0:T(4,128)S(1)}, s32[]{:T(128)}) %tuple.23), condition=%wide.while_cond, body=%wide.while_body.sunk | while | flops 2 | bytes 4201 | solution.py:112
  63.6 0.8 bitcast_dynamic-update-slice_fusion.2
  65.0 0.8 bitcast_dynamic-update-slice_fusion.2
  66.5 0.8 bitcast_dynamic-update-slice_fusion.2
  67.9 0.8 bitcast_dynamic-update-slice_fusion.2
  69.4 0.8 bitcast_dynamic-update-slice_fusion.2
  70.8 0.8 bitcast_dynamic-update-slice_fusion.2
  72.2 0.8 bitcast_dynamic-update-slice_fusion.2
  73.7 0.8 bitcast_dynamic-update-slice_fusion.2
  75.1 0.8 bitcast_dynamic-update-slice_fusion.2
  76.5 0.8 bitcast_dynamic-update-slice_fusion.2
  78.0 0.8 bitcast_dynamic-update-slice_fusion.2
  79.4 0.8 bitcast_dynamic-update-slice_fusion.2
  80.9 0.8 bitcast_dynamic-update-slice_fusion.2
  82.3 0.8 bitcast_dynamic-update-slice_fusion.2
  83.7 0.8 bitcast_dynamic-update-slice_fusion.2
  85.2 0.8 bitcast_dynamic-update-slice_fusion.2
  86.6 0.8 bitcast_dynamic-update-slice_fusion.2
  88.0 0.8 bitcast_dynamic-update-slice_fusion.2
  89.5 0.8 bitcast_dynamic-update-slice_fusion.2
  90.9 0.8 bitcast_dynamic-update-slice_fusion.2
  92.4 0.8 bitcast_dynamic-update-slice_fusion.2
  93.8 0.8 bitcast_dynamic-update-slice_fusion.2
  95.2 0.8 bitcast_dynamic-update-slice_fusion.2
  96.7 0.8 bitcast_dynamic-update-slice_fusion.2
  98.1 3.5 all-to-all-start.1
  101.5 27.6 %copy.79 = bf16[34,64,2560]{1,0,2:T(8,128)(2,1)} copy(bf16[34,64,2560]{2,1,0:T(8,128)(2,1)} %copy-done) | data formatting | bytes 22282240 | tf_op jit(solution)/shard_map/concatenate | solution.py:16
  129.2 30.5 %pad_maximum_fusion = bf16[34,64,2576]{1,0,2:T(8,128)(2,1)} fusion(bf16[34,64,8]{1,0,2:T(8,128)(2,1)S(1)} %copy.80, bf16[34,64,2560]{1,0,2:T(8,128)(2,1)} %copy.79, bf16[34,64,8]{1,0,2:T(8,128)(2,1)S(1)} %copy.78), kind=kLoop, calls=%fused_computation.7 | loop fusion | flops 11210752 | bytes 22421504 | tf_op jit(solution)/shard_map/concatenate | solution.py:16
  159.7 21.3 %gather_fusion = bf16[24,34,64,144]{2,1,3,0:T(8,128)(2,1)} fusion(bf16[34,64,2576]{1,0,2:T(8,128)(2,1)} %pad_maximum_fusion, s32[24]{0:T(128)S(1)} %get-tuple-element.30), kind=kCustom, calls=%fused_computation | custom fusion | bytes 30081312 | tf_op jit(solution)/shard_map/vmap()/gather | solution.py:107
  181.0 50.0 %copy.82 = bf16[24,34,64,144]{3,2,1,0:T(8,128)(2,1)} copy(bf16[24,34,64,144]{2,1,3,0:T(8,128)(2,1)} %gather_fusion) | data formatting | bytes 30081024 | tf_op jit(solution)/shard_map/vmap()/gather | solution.py:107
  231.1 6.8 all-to-all-start
  240.6 0.7 compare_and_fusion
  242.8 571.3 %all-to-all-done = bf16[24,34,64,144]{3,2,1,0:T(8,128)(2,1)} async-done(((bf16[24,34,64,144]{3,2,1,0:T(8,128)(2,1)}), bf16[24,34,64,144]{3,2,1,0:T(8,128)(2,1)}, u32[]{:S(2)}, u32[]{:S(2)}) %all-to-all-start) | async-done | bytes 15040544 | tf_op jit(solution)/shard_map/all_to_all | solution.py:119
  814.1 14.3 %gather_fusion.1 = bf16[10,34,64,144]{3,2,1,0:T(8,128)(2,1)} fusion(bf16[24,34,64,144]{3,2,1,0:T(8,128)(2,1)} %all-to-all-done, s32[1024]{0:T(1024)S(1)} %pad_clamp_fusion), kind=kCustom, calls=%fused_computation.1 | custom fusion | bytes 12533800 | tf_op jit(solution)/shard_map/jit(_take)/gather | solution.py:122
  828.4 16.4 %copy.83 = bf16[10,34,64,144]{2,3,1,0:T(8,128)(2,1)} copy(bf16[10,34,64,144]{3,2,1,0:T(8,128)(2,1)} %gather_fusion.1) | data formatting | bytes 12533760 | tf_op jit(solution)/shard_map/jit(_take)/gather | solution.py:122
  844.8 8.6 broadcast_select_fusion
  853.4 29.9 %fusion = f32[10,64,34,34,4]{1,0,4,3,2:T(8,128)} fusion(bf16[64,1,3,3,64]{0,4,3,2,1:T(8,128)(2,1)S(1)} %bitcast.67, bf16[10,34,64,36,4]{2,4,3,1,0:T(4,128)(2,1)S(1)} %broadcast_select_fusion), kind=kOutput, calls=%fused_computation.8 | convolution fusion | flops 2840985600 | bytes 18178048 | tf_op jit(solution)/shard_map/conv_general_dilated | solution.py:32
  883.3 131.4 %add_maximum_fusion = f32[10,64,32,32,4]{1,0,4,3,2:T(8,128)} fusion(f32[10,64,34,34,4]{1,0,4,3,2:T(8,128)} %fusion, f32[10,34,34]{0,2,1:T(8,128)S(1)} %copy.88, f32[64]{0:T(128)S(1)} %copy-done.6, f32[64]{0:T(128)S(1)} %copy-done.7, bf16[64,3,3,3,64]{4,3,2,1,0:T(4,128)(2,1)S(1)} %reshape.241), kind=kOutput, calls=%fused_computation.6 | convolution fusion | flops 7566827520 | bytes 22591136 | tf_op jit(solution)/shard_map/conv_general_dilated | solution.py:46
  1014.7 15.3 %reduce_sum.85 = f32[10,64,16,16,2]{1,0,4,3,2:T(8,128)} reduce(f32[10,64,16,2,16,2,2,2]{1,0,7,6,5,4,3,2:T(8,128)} %bitcast.65, f32[]{:T(128)} %constant.97.clone.1), dimensions={3,5,7}, to_apply=%region_9.10 | reduce | flops 2293760 | bytes 11796484 | tf_op jit(solution)/shard_map/reduce_sum | solution.py:58
  1030.0 3.8 fusion.6
  1033.8 1.3 copy.91
  1035.1 1.3 copy.92
  (106 shorter events, 22.4 us)
Async XLA Ops:
  0.0 37.1 %copy-start.4 = (s32[1,20]{1,0:T(1,128)S(1)}, s32[1,20]{1,0:T(1,128)}, u32[]{:S(2)}) copy-start(s32[1,20]{1,0:T(1,128)} %param.8) | copy-start | bytes 244
  0.0 37.3 %collective-permute-start.4 = (s32[1,20]{1,0:T(1,128)}, s32[1,20]{1,0:T(1,128)S(1)}, u32[]{:S(2)}, u32[]{:S(2)}) collective-permute-start(s32[1,20]{1,0:T(1,128)} %param.8), channel_id=1, source_target_pairs={{0,8},{8,16},{16,24},{1,9},{9,17},{17,25},{2,10},{10,18},{18,26},{... | collective-permute-start | bytes 248 | tf_op jit(solution)/shard_map/ppermute | solution.py:14
  2.5 34.8 %collective-permute-start.5 = (s32[1,20]{1,0:T(1,128)}, s32[1,20]{1,0:T(1,128)S(1)}, u32[]{:S(2)}, u32[]{:S(2)}) collective-permute-start(s32[1,20]{1,0:T(1,128)} %param.8), channel_id=1, source_target_pairs={{8,0},{16,8},{24,16},{9,1},{17,9},{25,17},{10,2},{18,10},{26,18},{... | collective-permute-start | bytes 248 | tf_op jit(solution)/shard_map/ppermute | solution.py:15
  30.3 4.0 copy-start.1
  34.4 12.0 %collective-permute-start = (bf16[1,64,2560]{2,1,0:T(8,128)(2,1)S(1)}, bf16[1,64,2560]{2,1,0:T(8,128)(2,1)S(1)}, u32[]{:S(2)}, u32[]{:S(2)}) collective-permute-start(bf16[1,64,2560]{2,1,0:T(8,128)(2,1)S(1)} %get-tuple-element.25), channel_id=1, source_target_pairs={{0,8},{8,16},{16,24},{1,9},{9,17},{17,25},{2,10},{10,18},{18,26},{... | collective-permute-start | bytes 983048 | tf_op jit(solution)/shard_map/ppermute | solution.py:14
  35.8 10.5 %collective-permute-start.1 = (bf16[1,64,2560]{2,1,0:T(8,128)(2,1)S(1)}, bf16[1,64,2560]{2,1,0:T(8,128)(2,1)S(1)}, u32[]{:S(2)}, u32[]{:S(2)}) collective-permute-start(bf16[1,64,2560]{2,1,0:T(8,128)(2,1)S(1)} %get-tuple-element.26), channel_id=1, source_target_pairs={{8,0},{16,8},{24,16},{9,1},{17,9},{25,17},{10,2},{18,10},{26,18},{... | collective-permute-start | bytes 983048 | tf_op jit(solution)/shard_map/ppermute | solution.py:15
  37.4 4.7 collective-permute-start.6
  40.8 5.5 collective-permute-start.7
  52.2 4.1 copy-start
  57.1 72.1 %collective-permute-start.3 = (bf16[34,64,8]{1,2,0:T(8,128)(2,1)S(1)}, bf16[34,64,8]{1,2,0:T(8,128)(2,1)S(1)}, u32[]{:S(2)}, u32[]{:S(2)}) collective-permute-start(bf16[34,64,8]{1,2,0:T(8,128)(2,1)S(1)} %copy.94), channel_id=1, source_target_pairs={{1,0},{2,1},{3,2},{4,3},{5,4},{6,5},{7,6},{9,8},{10,9},{11,10},{12... | collective-permute-start | bytes 104456 | tf_op jit(solution)/shard_map/ppermute | solution.py:15
  58.4 70.8 %collective-permute-start.2 = (bf16[34,64,8]{1,2,0:T(8,128)(2,1)S(1)}, bf16[34,64,8]{1,2,0:T(8,128)(2,1)S(1)}, u32[]{:S(2)}, u32[]{:S(2)}) collective-permute-start(bf16[34,64,8]{1,2,0:T(8,128)(2,1)S(1)} %copy.93), channel_id=1, source_target_pairs={{0,1},{1,2},{2,3},{3,4},{4,5},{5,6},{6,7},{8,9},{9,10},{10,11},{11... | collective-permute-start | bytes 104456 | tf_op jit(solution)/shard_map/ppermute | solution.py:14
  98.1 133.0 %all-to-all-start.1 = ((bf16[24,3,3]{2,1,0:T(4,128)(2,1)}), bf16[24,3,3]{2,1,0:T(4,128)(2,1)S(1)}, u32[]{:S(2)}, u32[]{:S(2)}) async-start(bf16[24,3,3]{2,1,0:T(4,128)(2,1)} %convert_element_type.55), calls=%async_computation.1 | async-start | bytes 49152 | tf_op jit(solution)/shard_map/all_to_all | solution.py:120
  231.1 6.9 copy-start.3
  231.1 7.0 copy-start.2
  231.1 7.4 copy-start.5
  231.1 583.1 %all-to-all-start = ((bf16[24,34,64,144]{3,2,1,0:T(8,128)(2,1)}), bf16[24,34,64,144]{3,2,1,0:T(8,128)(2,1)}, u32[]{:S(2)}, u32[]{:S(2)}) async-start(bf16[24,34,64,144]{3,2,1,0:T(8,128)(2,1)} %copy.82), calls=%async_computation | async-start | bytes 53477376 | tf_op jit(solution)/shard_map/all_to_all | solution.py:119
  853.4 29.9 %copy-start.6 = (f32[64]{0:T(128)S(1)}, f32[64]{0:T(128)}, u32[]{:S(2)}) copy-start(f32[64]{0:T(128)} %param.11) | copy-start | bytes 772
  853.4 29.9 %copy-start.7 = (f32[64]{0:T(128)S(1)}, f32[64]{0:T(128)}, u32[]{:S(2)}) copy-start(f32[64]{0:T(128)} %param.13) | copy-start | bytes 772
where the time goes:
time: 1040 us
  waiting for transfers between devices  575 us (55%)
  local copies, waits for them, and re-layouts  181 us (17%)
  matrix products  162 us (16%)
  other arithmetic  78.3 us (8%)
  starting transfers between devices  27.4 us (3%)
  blocking collectives  12.4 us (1%)
    all_to_all x1, waiting for transfers between devices, per_device(): lax.all_to_all(picked, 'xy', split_axis=0, concat_axis=0, tiled=True)  571 us
    conv_general_dilated x1, matrix products, conv_chain(): lax.conv_general_dilated(hidden, kernel_two, (1, 1, 1), ((0, 0), (0, 0),...  131 us
    gather x2, local copies, waits for them, and re-layouts, cut_brick(): lax.dynamic_slice_in_dim(full_rims, column_index * brick_span, (brick_sid...  71.4 us
    concatenate x4, other arithmetic, padded(): value = jnp.concatenate([before, value, after], axis=dim)  36.4 us
    gather x72, local copies, waits for them, and re-layouts  34.5 us
    gather x2, local copies, waits for them, and re-layouts, per_device(): chosen_bricks = jnp.take(arrived, arrival, axis=0)  30.7 us
    conv_general_dilated x1, matrix products, conv_chain(): lax.conv_general_dilated(extended, kernel_one, (1, 1, 1), ((0, 0), (0, 0)...  29.9 us
    concatenate x1, local copies, waits for them, and re-layouts, padded(): value = jnp.concatenate([before, value, after], axis=dim)  27.6 us
  transfers between devices with their start and end apart: 10, of which 2 were waited for; matrix products, arithmetic and copies ran while one was open for 18% of the time, Pallas kernels for 0%

commit v1 on v0

v1 whole, which is shorter than its diff:
```python
import functools

import numpy as np
import jax
import jax.numpy as jnp
from jax import lax
from jax.experimental import pallas as pl
from jax.experimental.pallas import tpu as pltpu
from jax.sharding import PartitionSpec as P

BF = jnp.bfloat16
F32 = jnp.float32
SIDE = 32
ACROSS = 4
PITCH = 40


def spread_matrix():
    table = np.zeros((ACROSS * PITCH, 256), np.float32)
    for x in range(ACROSS):
        for y in range(SIDE):
            table[x * PITCH + y + 2, y * ACROSS + x] = 1
        for y in range(2):
            table[x * PITCH + 34 + y, 128 + y * ACROSS + x] = 1
            table[x * PITCH + y, 128 + (30 + y) * ACROSS + x] = 1
    return table


def interleave_matrices():
    table = np.zeros((2, 256, 512), np.float32)
    for x in range(2):
        table[x, np.arange(256), np.arange(256) * 2 + x] = 1
    return table


def banded(taps):
    zero = jnp.zeros_like(taps[..., 0, :, :])
    rows = []
    for xi in range(ACROSS):
        blocks = []
        for xo in range(ACROSS):
            tap = xi - xo + 1
            blocks.append(taps[..., tap, :, :] if 0 <= tap < 3 else zero)
        rows.append(jnp.concatenate(blocks, axis=-1))
    return jnp.concatenate(rows, axis=-2)


def brick_kernel(
    n_ref, cols_ref, slots_ref, flags_ref,
    main_ref, prev_ref, next_ref, zmain_ref, zprev_ref, znext_ref, edge_ref,
    spread_ref, inter_ref, w1_ref, b1_ref, w2_ref, b2_ref,
    out_ref,
    ext_ref, hid_ref, taps_ref, pool_ref,
    *, columns,
):
    step = pl.program_id(0)

    @pl.when(step < n_ref[0])
    def _():
        col = cols_ref[step]
        first = col == 0
        last = col == columns - 1

        def flag(a, b):
            return flags_ref[step * 9 + 3 * a + b].astype(F32)

        lane = lax.broadcasted_iota(jnp.int32, (1, 1, 128), 2)
        low = lane < 64
        from_edge = jnp.where(low, last.astype(jnp.int32), first.astype(jnp.int32)) > 0

        def rim(before, after, edge, a):
            value = jnp.where(from_edge, edge, jnp.where(low, after, before))
            mask = jnp.where(low, flag(a, 2), flag(a, 0)).astype(BF)
            return value * mask

        spread = spread_ref[...]

        def put(own, side, first_layer):
            count = own.shape[0]
            both = jnp.concatenate(
                [own.reshape(count * 64, 128), side.reshape(count * 64, 128)], axis=1
            )
            turned = lax.dot_general(
                spread, both, (((1,), (1,)), ((), ())), preferred_element_type=F32
            )
            for k in range(count):
                for half in range(2):
                    pieces = [
                        turned[x * PITCH:(x + 1) * PITCH, k * 64:(k + 1) * 64]
                        for x in (2 * half, 2 * half + 1)
                    ]
                    ext_ref[first_layer + k, 0:PITCH, half * 128:(half + 1) * 128] = (
                        jnp.concatenate(pieces, axis=1)
                    )

        def main_layers(k, carry):
            z = pl.multiple_of(k * 4, 4)
            at = pl.ds(z, 4)
            side = rim(prev_ref[at], next_ref[at], edge_ref[at], 1)
            put(main_ref[at], side, z + 1)
            return carry

        lax.fori_loop(0, 8, main_layers, 0)
        for layer, a, spot in ((0, 0, 0), (1, 2, 33)):
            at = slice(layer, layer + 1)
            side = rim(zprev_ref[at], znext_ref[at], edge_ref[32 + layer:33 + layer], a)
            put(zmain_ref[at] * flag(a, 1).astype(BF), side, spot)

        y_at = lax.broadcasted_iota(jnp.int32, (1, PITCH, 256), 1)

        def region(a):
            return jnp.where(
                y_at == 0, flag(a, 0), jnp.where(y_at == 33, flag(a, 2), flag(a, 1))
            )

        bias_one = b1_ref[...]

        def first_conv(z, count, a):
            at = pl.ds(z, count)
            rows = [
                ext_ref[at, t:t + PITCH, :].reshape(count * PITCH, 256).astype(BF)
                for t in range(3)
            ]
            total = jnp.dot(
                jnp.concatenate(rows, axis=1), w1_ref[...], preferred_element_type=F32
            )
            act = jnp.maximum(total + bias_one, 0.0).reshape(count, PITCH, 256)
            hid_ref[0:count] = act * region(a)
            for t in range(3):
                taps_ref[at, :, t * 256:(t + 1) * 256] = hid_ref[
                    0:count, t:t + SIDE, :
                ].astype(BF)

        first_conv(0, 1, 0)
        lax.fori_loop(0, 4, lambda k, c: (first_conv(k * 8 + 1, 8, 1), c)[1], 0)
        first_conv(33, 1, 2)

        bias_two = b2_ref[...]

        def second_conv(k, carry):
            z = k * 8
            total = jnp.zeros((8 * SIDE, 256), F32)
            for a in range(3):
                rows = taps_ref[pl.ds(z + a, 8)].reshape(8 * SIDE, 768)
                total = total + jnp.dot(rows, w2_ref[a], preferred_element_type=F32)
            act = jnp.maximum(total + bias_two, 0.0).reshape(4, 2, SIDE, 256)
            act = act[:, 0] + act[:, 1]
            left, right = act[..., :128], act[..., 128:]
            left = left + pltpu.roll(left, 64, 2)
            right = right + pltpu.roll(right, 64, 2)
            pool_ref[pl.ds(k * 4, 4)] = jnp.where(low, left, right)
            return carry

        lax.fori_loop(0, 4, second_conv, 0)
        pooled = pool_ref[:, pl.ds(0, 16, stride=2), :] + pool_ref[:, pl.ds(1, 16, stride=2), :]
        pooled = (pooled * 0.125).reshape(256, 128)
        turned = jnp.transpose(pooled).astype(BF)
        result = jnp.dot(turned[:64], inter_ref[0], preferred_element_type=F32)
        result = result + jnp.dot(turned[64:], inter_ref[1], preferred_element_type=F32)
        out_ref[0] = result.astype(BF)


def compute_bricks(
    count, cols, slots, flags, volume, zhalo, edge, w1, b1, w2, b2, out_slots, columns
):
    spread = jnp.asarray(spread_matrix(), BF)
    inter = jnp.asarray(interleave_matrices(), BF)

    def at(shift):
        def index(i, n, c, s, f):
            return (0, 0, jnp.clip(c[i] + shift, 0, columns - 1))
        return index

    def whole(shape):
        return pl.BlockSpec(shape, lambda i, n, c, s, f: (0,) * len(shape))

    grid_spec = pltpu.PrefetchScalarGridSpec(
        num_scalar_prefetch=4,
        grid=(columns,),
        in_specs=[pl.BlockSpec((SIDE, 64, 128), at(s)) for s in (0, -1, 1)]
        + [pl.BlockSpec((2, 64, 128), at(s)) for s in (0, -1, 1)]
        + [whole(v.shape) for v in (edge, spread, inter, w1, b1, w2, b2)],
        out_specs=pl.BlockSpec((1, 64, 512), lambda i, n, c, s, f: (s[i], 0, 0)),
        scratch_shapes=[
            pltpu.VMEM((34, 48, 256), F32),
            pltpu.VMEM((8, PITCH, 256), F32),
            pltpu.VMEM((34, SIDE, 768), BF),
            pltpu.VMEM((16, SIDE, 128), F32),
        ],
    )
    return pl.pallas_call(
        functools.partial(brick_kernel, columns=columns),
        out_shape=jax.ShapeDtypeStruct((out_slots, 64, 512), BF),
        grid_spec=grid_spec,
        compiler_params=pltpu.CompilerParams(
            dimension_semantics=("arbitrary",), vmem_limit_bytes=48 * 1024 * 1024
        ),
        cost_estimate=pl.CostEstimate(
            flops=columns * 1_600_000_000, bytes_accessed=columns * 1_600_000, transcendentals=0
        ),
    )(count, cols, slots, flags, volume, volume, volume, zhalo, zhalo, zhalo, edge,
      spread, inter, w1, b1, w2, b2)


def per_device(volume, occupancy, device_order, weight_one, bias_one, weight_two, bias_two):
    columns = occupancy.shape[1]
    slabs = lax.axis_size("gz")
    groups = lax.axis_size("xy")
    capacity = (columns + groups - 1) // groups
    slot_count = columns // 2
    me_z = lax.axis_index("gz")
    me = lax.axis_index("xy")
    rims = 2 * ACROSS

    up_z = [(i, i + 1) for i in range(slabs - 1)]
    down_z = [(j, i) for i, j in up_z]
    up_y = [(i, i + 1) for i in range(groups - 1)]
    down_y = [(j, i) for i, j in up_y]
    below = lax.ppermute(volume[SIDE - 1:], "gz", up_z)
    above = lax.ppermute(volume[:1], "gz", down_z)
    zhalo = jnp.concatenate([below, above], axis=0)
    span = volume.shape[2]
    tail = jnp.concatenate([volume[:, :, span - rims:], zhalo[:, :, span - rims:]], axis=0)
    head = jnp.concatenate([volume[:, :, :rims], zhalo[:, :, :rims]], axis=0)
    layers = tail.shape[0]
    before = lax.ppermute(tail.reshape(layers, -1), "xy", up_y).reshape(layers, 64, rims)
    after = lax.ppermute(head.reshape(layers, -1), "xy", down_y).reshape(layers, 64, rims)
    edge = jnp.concatenate(
        [after, jnp.zeros((layers, 64, 128 - 2 * rims), BF), before], axis=2
    )

    table = lax.all_gather(occupancy, ("gz", "xy"), axis=0, tiled=True)
    table = table.reshape(slabs, groups * columns)
    total = groups * columns
    marks = jnp.pad(table, ((1, 1), (1, 1)))
    near = lax.dynamic_slice(marks, (me_z, me * columns), (3, columns + 2))
    row = lax.dynamic_slice(table, (me_z, 0), (1, total))[0]
    own = occupancy[0]
    order = device_order[0]
    ids = jnp.arange(columns, dtype=jnp.int32)
    labels = jnp.arange(groups, dtype=jnp.int32)
    everyone = jnp.arange(total, dtype=jnp.int32)
    local_rank = jnp.sum(jnp.where(ids[None, :] < ids[:, None], own[None, :], 0), axis=1)
    start = jnp.sum(jnp.where(everyone < me * columns, row, 0))
    label = (start + local_rank) % groups
    target = jnp.sum(jnp.where(label[:, None] == labels[None, :], order[None, :], 0), axis=1)
    slot = target * capacity + local_rank // groups
    count = jnp.sum(own)
    wanted = jnp.minimum(ids, jnp.maximum(count - 1, 0))
    hit = (local_rank[None, :] == wanted[:, None]) & (own[None, :] > 0)
    cols = jnp.sum(jnp.where(hit, ids[None, :], 0), axis=1)
    slots = jnp.sum(jnp.where(hit, slot[None, :], 0), axis=1)
    flag_of = jnp.stack([near[a, b:b + columns] for a in range(3) for b in range(3)], axis=1)
    flags = jnp.sum(jnp.where(hit[:, :, None], flag_of[None], 0), axis=1).reshape(-1)

    w1 = banded(weight_one.reshape(64, 3, 3, 64).transpose(1, 2, 3, 0)).reshape(768, 256)
    w2 = banded(weight_two.reshape(64, 3, 3, 3, 64).transpose(1, 2, 3, 4, 0)).reshape(3, 768, 256)
    b1 = jnp.tile(bias_one, ACROSS)[None]
    b2 = jnp.tile(bias_two, ACROSS)[None]

    made = compute_bricks(
        count.reshape(1), cols, slots, flags, volume, zhalo, edge, w1, b1, w2, b2,
        groups * capacity, columns,
    )
    arrived = lax.all_to_all(made, "xy", split_axis=0, concat_axis=0, tiled=True)

    my_label = jnp.sum(jnp.where(order == me, labels, 0))
    need = jnp.arange(slot_count, dtype=jnp.int32) * groups + my_label
    counts = row.reshape(groups, columns).sum(axis=1)
    starts = jnp.sum(jnp.where(labels[None, :] < labels[:, None], counts[None, :], 0), axis=1)
    owner = jnp.sum(((starts + counts)[None, :] <= need[:, None]).astype(jnp.int32), axis=1)
    owner_start = jnp.sum(jnp.where(labels[None, :] == owner[:, None], starts[None, :], 0), axis=1)
    arrival = owner * capacity + (need - owner_start) // groups
    return jnp.take(arrived, arrival, axis=0)


def solution(mesh):
    in_specs = (P("gz", None, "xy"), P("gz", "xy"), P("gz", None), P(), P(), P(), P())
    out_specs = P(("gz", "xy"), None, None)
    return jax.shard_map(
        per_device, mesh=mesh, in_specs=in_specs, out_specs=out_specs, check_vma=False
    )
```

time: 1040 us -> 293 us (0.28)
  waiting for transfers between devices: 575 us -> 29.6 us
  local copies, waits for them, and re-layouts: 181 us -> 17.7 us
  matrix products: 162 us -> 0 us
  starting transfers between devices: 27.4 us -> 111 us
  other arithmetic: 78.3 us -> 14.2 us
  blocking collectives: 12.4 us -> 70.1 us
  Pallas kernels: 0 us -> 48 us
    all_to_all x2 -> x1, waiting for transfers between devices: 571 us -> 29.5 us  [per_device(): lax.all_to_all(made, 'xy', split_axis=0, concat_axis=0, tiled=True)]
    conv_general_dilated x2 -> x0, matrix products: 161 us -> none  [the longest x1 131 us: conv_chain(): lax.conv_general_dilated(hidden, kernel_two, (1, 1, 1), ((0, 0), (0, 0),...]
    gather x77 -> x1, local copies, waits for them, and re-layouts: 137 us -> 0.59 us  [per_device(): return jnp.take(arrived, arrival, axis=0)]
    all_to_all x2 -> x1, starting transfers between devices: 10.3 us -> 100 us  [per_device(): lax.all_to_all(made, 'xy', split_axis=0, concat_axis=0, tiled=True)]
    all_gather x0 -> x1, blocking collectives: none -> 70.1 us  [per_device(): table = lax.all_gather(occupancy, ('gz', 'xy'), axis=0, tiled=True)]
    pallas_call x0 -> x1, Pallas kernels: none -> 48 us  [compute_bricks(): pl.pallas_call(functools.partial(brick_kernel, columns=columns), out_shap...]
    concatenate x4, other arithmetic: 36.4 us -> 6.95 us  [the longest x2 3.49 us: banded(): return jnp.concatenate(rows, axis=-2)]
    concatenate x2 -> x4, local copies, waits for them, and re-layouts: 27.6 us -> 4.25 us  [the longest x1 1.78 us: per_device(): head = jnp.concatenate([volume[:, :, :rims], zhalo[:, :, :rims]], axis=0)]
  transfers between devices with their start and end apart: 10 -> 5, of which waited for: 2 -> 1; matrix products, arithmetic and copies ran while one was open for 18% -> 7% of each run, Pallas kernels for 0% -> 0%
where the time goes in v1:
time: 293 us; the launch traced here: 291 us
  starting transfers between devices  111 us (38%)
  blocking collectives  70.1 us (24%)
  Pallas kernels  48 us (16%)
  waiting for transfers between devices  29.6 us (10%)
  local copies, waits for them, and re-layouts  17.7 us (6%)
  other arithmetic  14.2 us (5%)
    all_to_all x1, starting transfers between devices, per_device(): lax.all_to_all(made, 'xy', split_axis=0, concat_axis=0, tiled=True)  100 us
    all_gather x1, blocking collectives, per_device(): table = lax.all_gather(occupancy, ('gz', 'xy'), axis=0, tiled=True)  70.1 us
    pallas_call x1, Pallas kernels, compute_bricks(): pl.pallas_call(functools.partial(brick_kernel, columns=columns), out_shap...  48 us
    all_to_all x1, waiting for transfers between devices, per_device(): lax.all_to_all(made, 'xy', split_axis=0, concat_axis=0, tiled=True)  29.5 us
  transfers between devices with their start and end apart: 5, of which 1 were waited for; matrix products, arithmetic and copies ran while one was open for 7% of the time, Pallas kernels for 0%

profile of v1, /device:TPU:0, one launch (start us, length us, event | category | flops | bytes accessed | tf_op | source)
XLA Modules:
  0.0 291.5 jit_solution(988187726459347700)
XLA Ops:
  0.0 1.2 fusion.7
  1.2 3.1 %collective-permute-start = (bf16[1,64,2560]{2,1,0:T(8,128)(2,1)S(1)}, bf16[1,64,2560]{2,1,0:T(8,128)(2,1)}, u32[]{:S(2)}, u32[]{:S(2)}) collective-permute-start(bf16[1,64,2560]{2,1,0:T(8,128)(2,1)S(1)} %get-tuple-element.13), channel_id=1, source_target_pairs={{0,8},{8,16},{16,24},{1,9},{9,17},{17,25},{2,10},{10,18},{18,26},{... | collective-permute-start | bytes 983048 | tf_op jit(solution)/shard_map/ppermute | solution.py:219
  4.3 1.3 collective-permute-start.1
  5.5 2.3 fusion.6
  7.8 0.7 reduce_sum.115
  8.5 70.1 %all-gather = s32[32,1,20]{2,1,0:T(1,128)S(1)} all-gather(s32[1,1,20]{2,1,0:T(1,128)S(1)} %bitcast.69), channel_id=1, replica_groups=mesh['gz'=4,'xy'=8] {'gz','xy'}, dimensions={0}, use_global_device_ids=true | all-gather | bytes 2640 | tf_op jit(solution)/shard_map/all_gather | solution.py:232
  78.6 0.5 broadcast.311
  79.1 0.7 reduce.7
  79.8 0.1 reshape.214
  79.9 0.1 pad_dynamic-slice_fusion
  79.9 0.1 slice_bitcast_fusion.3
  80.0 0.7 fusion.5
  80.7 0.6 fusion
  81.3 0.1 select_reduce_fusion.3
  82.1 0.0 copy-done.2
  82.1 0.3 reshape.223
  82.4 0.6 fusion.9
  83.1 0.2 copy.89
  83.2 0.2 copy.90
  83.4 0.2 copy.91
  83.6 0.1 copy.86
  83.7 0.7 and_select_fusion.2
  84.4 0.1 select_reduce_fusion.4
  84.5 0.2 select_reduce_fusion.1
  84.7 0.2 maximum_maximum_fusion.1
  85.0 3.3 %maximum_maximum_fusion = bf16[3,3,256,256]{3,2,1,0:T(8,128)(2,1)S(1)} fusion(bf16[3,3,64,64]{3,2,1,0:T(8,128)(2,1)S(1)} %bitcast.63, bf16[3,3,64,64]{3,2,1,0:T(8,128)(2,1)S(1)} %bitcast.65, bf16[3,3,64,128]{3,2,1,0:T(8,128)(2,1)S(1)} %broadcast.278, bf16[3,3,64,64]{3,2,1,0:T(8,128)(2,1)S(1)} %bitcast.64, bf16[3,3,64,64]{3,2,1,0:T(8,128)(2,1)S(1)} %broadcast_in_dim.143), kind=kLoop, calls=%fused_computation.1 | loop fusion | flops 16515072 | bytes 1622016 | tf_op jit(solution)/shard_map/concatenate | solution.py:45
  88.3 0.0 collective-permute-done
  88.3 1.0 constant_dynamic-update-slice_fusion.1
  89.3 0.0 copy-start.5
  89.3 0.0 copy-start.6
  89.4 0.0 collective-permute-done.1
  89.4 1.0 constant_dynamic-update-slice_fusion.zmain_ref.zprev_ref.znext_ref
  90.4 0.1 fusion.8
  90.5 2.1 pad_maximum_fusion
  92.5 1.8 copy.82
  94.3 1.3 collective-permute-start.2
  95.6 1.4 copy.83
  97.0 5.2 %collective-permute-start.3 = (bf16[34,512]{0,1:T(8,128)(2,1)}, bf16[34,512]{0,1:T(8,128)(2,1)}, u32[]{:S(2)}, u32[]{:S(2)}) collective-permute-start(bf16[34,512]{0,1:T(8,128)(2,1)} %bitcast.67), channel_id=1, source_target_pairs={{0,1},{1,2},{2,3},{3,4},{4,5},{5,6},{6,7},{8,9},{9,10},{10,11},{11... | collective-permute-start | bytes 104456 | tf_op jit(solution)/shard_map/ppermute | solution.py:226
  102.2 0.2 select_reduce_fusion
  102.4 0.1 copy.81
  102.5 0.1 reshape.216.flags_ref
  102.6 0.0 copy-done.5
  102.6 0.1 broadcast_in_dim_tile.6.b1_ref
  102.7 0.1 broadcast_in_dim_tile.7.b2_ref
  102.8 0.1 pad.34.clone
  102.9 0.0 collective-permute-done.2
  102.9 2.0 copy.84
  104.9 0.0 collective-permute-done.3
  104.9 2.8 copy.85
  107.7 1.4 pad_maximum_fusion.2.edge_ref
  109.1 48.0 %shard_map.91 = bf16[24,64,512]{2,1,0:T(8,128)(2,1)} custom-call(s32[1]{0:T(128)} %bitcast.2.n_ref, s32[20]{0:T(128)S(1)} %get-tuple-element.6.cols_ref, s32[20]{0:T(128)S(1)} %get-tuple-element.5.slots_ref, s32[180]{0:T(256)S(1)} %reshape.216.flags_ref, bf16[32,64,2560]{2,1,0:T(8,128)(2,1)} %next_ref.1, bf16[32,64,2560]{2,1,0:T(8,128)(2,1)} %next_ref.1, ...), custom_call_target="tpu_custom_call" | custom-call | flops 32000000000 | bytes 32000000 | tf_op jit(solution)/shard_map/pallas_call | solution.py:191
  157.1 100.1 %all-to-all-start = ((bf16[24,64,512]{2,1,0:T(8,128)(2,1)}), bf16[24,64,512]{2,1,0:T(8,128)(2,1)S(1)}, u32[]{:S(2)}, u32[]{:S(2)}) async-start(bf16[24,64,512]{2,1,0:T(8,128)(2,1)} %shard_map.91), calls=%async_computation | async-start | bytes 3145728 | tf_op jit(solution)/shard_map/all_to_all | solution.py:265
  257.2 0.1 reshape_squeeze.3
  257.3 0.1 reduce_sum.110
  257.4 0.1 select_reduce_fusion.6
  257.6 0.6 fusion.1
  258.2 0.6 multiply_add_fusion
  258.9 0.1 convert_reduce_fusion
  258.9 0.1 select_reduce_fusion.5
  259.0 0.7 fusion.3
  259.7 0.7 compare_and_fusion.1
  260.4 29.5 %all-to-all-done = bf16[24,64,512]{2,1,0:T(8,128)(2,1)S(1)} async-done(((bf16[24,64,512]{2,1,0:T(8,128)(2,1)}), bf16[24,64,512]{2,1,0:T(8,128)(2,1)S(1)}, u32[]{:S(2)}, u32[]{:S(2)}) %all-to-all-start) | async-done | bytes 1572896 | tf_op jit(solution)/shard_map/all_to_all | solution.py:265
  289.9 0.6 gather_fusion
  290.5 1.0 broadcast_select_fusion
  (27 shorter events, 0.2 us)
Async XLA Ops:
  0.0 7.8 %copy-start.4 = (s32[1,20]{1,0:T(1,128)S(1)}, s32[1,20]{1,0:T(1,128)}, u32[]{:S(2)}) copy-start(s32[1,20]{1,0:T(1,128)} %param.10) | copy-start | bytes 244
  0.0 82.1 %copy-start.2 = (bf16[64,1728]{1,0:T(8,128)(2,1)S(1)}, bf16[64,1728]{1,0:T(8,128)(2,1)}, u32[]{:S(2)}) copy-start(bf16[64,1728]{1,0:T(8,128)(2,1)} %param.14) | copy-start | bytes 663556
  1.2 87.2 %collective-permute-start = (bf16[1,64,2560]{2,1,0:T(8,128)(2,1)S(1)}, bf16[1,64,2560]{2,1,0:T(8,128)(2,1)}, u32[]{:S(2)}, u32[]{:S(2)}) collective-permute-start(bf16[1,64,2560]{2,1,0:T(8,128)(2,1)S(1)} %get-tuple-element.13), channel_id=1, source_target_pairs={{0,8},{8,16},{16,24},{1,9},{9,17},{17,25},{2,10},{10,18},{18,26},{... | collective-permute-start | bytes 983048 | tf_op jit(solution)/shard_map/ppermute | solution.py:219
  4.3 85.1 %collective-permute-start.1 = (bf16[1,64,2560]{2,1,0:T(8,128)(2,1)S(1)}, bf16[1,64,2560]{2,1,0:T(8,128)(2,1)}, u32[]{:S(2)}, u32[]{:S(2)}) collective-permute-start(bf16[1,64,2560]{2,1,0:T(8,128)(2,1)S(1)} %get-tuple-element.12), channel_id=1, source_target_pairs={{8,0},{16,8},{24,16},{9,1},{17,9},{25,17},{10,2},{18,10},{26,18},{... | collective-permute-start | bytes 983048 | tf_op jit(solution)/shard_map/ppermute | solution.py:220
  7.8 75.8 %copy-start.3 = (bf16[64,576]{1,0:T(8,128)(2,1)S(1)}, bf16[64,576]{1,0:T(8,128)(2,1)}, u32[]{:S(2)}) copy-start(bf16[64,576]{1,0:T(8,128)(2,1)} %param.12) | copy-start | bytes 221188
  7.8 76.6 %copy-start.7 = (s32[1,8]{1,0:T(1,128)S(1)}, s32[1,8]{1,0:T(1,128)}, u32[]{:S(2)}) copy-start(s32[1,8]{1,0:T(1,128)} %param.11) | copy-start | bytes 100
  89.3 13.3 %copy-start.5 = (f32[64]{0:T(128)S(1)}, f32[64]{0:T(128)}, u32[]{:S(2)}) copy-start(f32[64]{0:T(128)} %param.13) | copy-start | bytes 772
  89.3 13.4 %copy-start.6 = (f32[64]{0:T(128)S(1)}, f32[64]{0:T(128)}, u32[]{:S(2)}) copy-start(f32[64]{0:T(128)} %param.15) | copy-start | bytes 772
  92.5 16.5 %copy-start = (bf16[2,256,512]{2,1,0:T(8,128)(2,1)S(1)}, bf16[2,256,512]{2,1,0:T(8,128)(2,1)}, u32[]{:S(2)}) copy-start(bf16[2,256,512]{2,1,0:T(8,128)(2,1)} %constant.86.clone.inter_ref) | copy-start | bytes 1572868
  92.5 16.6 %copy-start.1 = (bf16[160,256]{1,0:T(8,128)(2,1)S(1)}, bf16[160,256]{1,0:T(8,128)(2,1)}, u32[]{:S(2)}) copy-start(bf16[160,256]{1,0:T(8,128)(2,1)} %constant.85.clone.spread_ref) | copy-start | bytes 245764
  94.3 8.6 %collective-permute-start.2 = (bf16[34,512]{0,1:T(8,128)(2,1)S(1)}, bf16[34,512]{0,1:T(8,128)(2,1)}, u32[]{:S(2)}, u32[]{:S(2)}) collective-permute-start(bf16[34,512]{0,1:T(8,128)(2,1)S(1)} %bitcast.66), channel_id=1, source_target_pairs={{1,0},{2,1},{3,2},{4,3},{5,4},{6,5},{7,6},{9,8},{10,9},{11,10},{12... | collective-permute-start | bytes 104456 | tf_op jit(solution)/shard_map/ppermute | solution.py:227
  97.0 7.9 %collective-permute-start.3 = (bf16[34,512]{0,1:T(8,128)(2,1)}, bf16[34,512]{0,1:T(8,128)(2,1)}, u32[]{:S(2)}, u32[]{:S(2)}) collective-permute-start(bf16[34,512]{0,1:T(8,128)(2,1)} %bitcast.67), channel_id=1, source_target_pairs={{0,1},{1,2},{2,3},{3,4},{4,5},{5,6},{6,7},{8,9},{9,10},{10,11},{11... | collective-permute-start | bytes 104456 | tf_op jit(solution)/shard_map/ppermute | solution.py:226
  157.1 100.5 %copy-start.8 = (s32[1,8]{1,0:T(1,128)S(1)}, s32[1,8]{1,0:T(1,128)}, u32[]{:S(2)}) copy-start(s32[1,8]{1,0:T(1,128)} %param.11) | copy-start | bytes 100
  157.1 132.8 %all-to-all-start = ((bf16[24,64,512]{2,1,0:T(8,128)(2,1)}), bf16[24,64,512]{2,1,0:T(8,128)(2,1)S(1)}, u32[]{:S(2)}, u32[]{:S(2)}) async-start(bf16[24,64,512]{2,1,0:T(8,128)(2,1)} %shard_map.91), calls=%async_computation | async-start | bytes 3145728 | tf_op jit(solution)/shard_map/all_to_all | solution.py:265

commit v2 on v1

--- a/solution.py
+++ b/solution.py
@@ -93,65 +93,70 @@
                         jnp.concatenate(pieces, axis=1)
                     )
 
-        def main_layers(k, carry):
-            z = pl.multiple_of(k * 4, 4)
-            at = pl.ds(z, 4)
-            side = rim(prev_ref[at], next_ref[at], edge_ref[at], 1)
-            put(main_ref[at], side, z + 1)
-            return carry
-
-        lax.fori_loop(0, 8, main_layers, 0)
-        for layer, a, spot in ((0, 0, 0), (1, 2, 33)):
+        def put_main(k):
+            at = slice(4 * k, 4 * k + 4)
+            put(main_ref[at], rim(prev_ref[at], next_ref[at], edge_ref[at], 1), 4 * k + 1)
+
+        def put_rim(layer, a, spot):
             at = slice(layer, layer + 1)
             side = rim(zprev_ref[at], znext_ref[at], edge_ref[32 + layer:33 + layer], a)
             put(zmain_ref[at] * flag(a, 1).astype(BF), side, spot)
 
-        y_at = lax.broadcasted_iota(jnp.int32, (1, PITCH, 256), 1)
-
-        def region(a):
-            return jnp.where(
-                y_at == 0, flag(a, 0), jnp.where(y_at == 33, flag(a, 2), flag(a, 1))
-            )
-
+        y_at = lax.broadcasted_iota(jnp.int32, (PITCH, 256), 0)
+        regions = [
+            jnp.where(y_at == 0, flag(a, 0), jnp.where(y_at == 33, flag(a, 2), flag(a, 1)))
+            for a in range(3)
+        ]
         bias_one = b1_ref[...]
-
-        def first_conv(z, count, a):
-            at = pl.ds(z, count)
+        bias_two = b2_ref[...]
+
+        def first_conv(z, count):
             rows = [
-                ext_ref[at, t:t + PITCH, :].reshape(count * PITCH, 256).astype(BF)
+                ext_ref[z:z + count, t:t + PITCH, :].reshape(count * PITCH, 256).astype(BF)
                 for t in range(3)
             ]
             total = jnp.dot(
                 jnp.concatenate(rows, axis=1), w1_ref[...], preferred_element_type=F32
             )
             act = jnp.maximum(total + bias_one, 0.0).reshape(count, PITCH, 256)
-            hid_ref[0:count] = act * region(a)
+            for k in range(count):
+                zone = 0 if z + k == 0 else 2 if z + k == 33 else 1
+                hid_ref[z + k] = act[k] * regions[zone]
             for t in range(3):
-                taps_ref[at, :, t * 256:(t + 1) * 256] = hid_ref[
-                    0:count, t:t + SIDE, :
+                taps_ref[z:z + count, :, t * 256:(t + 1) * 256] = hid_ref[
+                    z:z + count, t:t + SIDE, :
                 ].astype(BF)
 
-        first_conv(0, 1, 0)
-        lax.fori_loop(0, 4, lambda k, c: (first_conv(k * 8 + 1, 8, 1), c)[1], 0)
-        first_conv(33, 1, 2)
-
-        bias_two = b2_ref[...]
-
-        def second_conv(k, carry):
-            z = k * 8
-            total = jnp.zeros((8 * SIDE, 256), F32)
-            for a in range(3):
-                rows = taps_ref[pl.ds(z + a, 8)].reshape(8 * SIDE, 768)
-                total = total + jnp.dot(rows, w2_ref[a], preferred_element_type=F32)
+        def second_conv(z):
+            rows = [taps_ref[z + a:z + a + 8].reshape(8 * SIDE, 768) for a in range(3)]
+            total = jnp.dot(
+                jnp.concatenate(rows, axis=1), w2_ref[...], preferred_element_type=F32
+            )
             act = jnp.maximum(total + bias_two, 0.0).reshape(4, 2, SIDE, 256)
             act = act[:, 0] + act[:, 1]
             left, right = act[..., :128], act[..., 128:]
             left = left + pltpu.roll(left, 64, 2)
             right = right + pltpu.roll(right, 64, 2)
-            pool_ref[pl.ds(k * 4, 4)] = jnp.where(low, left, right)
-            return carry
-
-        lax.fori_loop(0, 4, second_conv, 0)
+            pool_ref[z // 2:z // 2 + 4] = jnp.where(low, left, right)
+
+        put_rim(0, 0, 0)
+        put_main(0)
+        put_main(1)
+        first_conv(0, 9)
+        put_main(2)
+        put_main(3)
+        first_conv(9, 8)
+        second_conv(0)
+        put_main(4)
+        put_main(5)
+        first_conv(17, 8)
+        second_conv(8)
+        put_main(6)
+        put_main(7)
+        put_rim(1, 2, 33)
+        first_conv(25, 9)
+        second_conv(16)
+        second_conv(24)
         pooled = pool_ref[:, pl.ds(0, 16, stride=2), :] + pool_ref[:, pl.ds(1, 16, stride=2), :]
         pooled = (pooled * 0.125).reshape(256, 128)
         turned = jnp.transpose(pooled).astype(BF)
@@ -161,7 +166,7 @@
 
 
 def compute_bricks(
-    count, cols, slots, flags, volume, zhalo, edge, w1, b1, w2, b2, out_slots, columns
+    count, cols, slots, flags, volume, zhalo, edge, w1, b1, w2, b2, out_slots, columns, steps
 ):
     spread = jnp.asarray(spread_matrix(), BF)
     inter = jnp.asarray(interleave_matrices(), BF)
@@ -176,14 +181,14 @@
 
     grid_spec = pltpu.PrefetchScalarGridSpec(
         num_scalar_prefetch=4,
-        grid=(columns,),
+        grid=(steps,),
         in_specs=[pl.BlockSpec((SIDE, 64, 128), at(s)) for s in (0, -1, 1)]
         + [pl.BlockSpec((2, 64, 128), at(s)) for s in (0, -1, 1)]
         + [whole(v.shape) for v in (edge, spread, inter, w1, b1, w2, b2)],
         out_specs=pl.BlockSpec((1, 64, 512), lambda i, n, c, s, f: (s[i], 0, 0)),
         scratch_shapes=[
             pltpu.VMEM((34, 48, 256), F32),
-            pltpu.VMEM((8, PITCH, 256), F32),
+            pltpu.VMEM((34, PITCH, 256), F32),
             pltpu.VMEM((34, SIDE, 768), BF),
             pltpu.VMEM((16, SIDE, 128), F32),
         ],
@@ -196,7 +201,7 @@
             dimension_semantics=("arbitrary",), vmem_limit_bytes=48 * 1024 * 1024
         ),
         cost_estimate=pl.CostEstimate(
-            flops=columns * 1_600_000_000, bytes_accessed=columns * 1_600_000, transcendentals=0
+            flops=steps * 1_600_000_000, bytes_accessed=steps * 1_600_000, transcendentals=0
         ),
     )(count, cols, slots, flags, volume, volume, volume, zhalo, zhalo, zhalo, edge,
       spread, inter, w1, b1, w2, b2)
@@ -244,25 +249,39 @@
     start = jnp.sum(jnp.where(everyone < me * columns, row, 0))
     label = (start + local_rank) % groups
     target = jnp.sum(jnp.where(label[:, None] == labels[None, :], order[None, :], 0), axis=1)
-    slot = target * capacity + local_rank // groups
     count = jnp.sum(own)
-    wanted = jnp.minimum(ids, jnp.maximum(count - 1, 0))
-    hit = (local_rank[None, :] == wanted[:, None]) & (own[None, :] > 0)
-    cols = jnp.sum(jnp.where(hit, ids[None, :], 0), axis=1)
-    slots = jnp.sum(jnp.where(hit, slot[None, :], 0), axis=1)
     flag_of = jnp.stack([near[a, b:b + columns] for a in range(3) for b in range(3)], axis=1)
-    flags = jnp.sum(jnp.where(hit[:, :, None], flag_of[None], 0), axis=1).reshape(-1)
+    early = min(columns, 2 * groups)
+
+    def part(begin, end):
+        amount = jnp.clip(count - begin, 0, end - begin)
+        wanted = begin + jnp.minimum(
+            jnp.arange(end - begin, dtype=jnp.int32), jnp.maximum(amount - 1, 0)
+        )
+        hit = (local_rank[None, :] == wanted[:, None]) & (own[None, :] > 0)
+        cols = jnp.sum(jnp.where(hit, ids[None, :], 0), axis=1)
+        part_capacity = (end - begin + groups - 1) // groups
+        slot = target * part_capacity + (local_rank - begin) // groups
+        slots = jnp.sum(jnp.where(hit, slot[None, :], 0), axis=1)
+        flags = jnp.sum(jnp.where(hit[:, :, None], flag_of[None], 0), axis=1).reshape(-1)
+        return amount.reshape(1), cols, slots, flags, part_capacity
 
     w1 = banded(weight_one.reshape(64, 3, 3, 64).transpose(1, 2, 3, 0)).reshape(768, 256)
-    w2 = banded(weight_two.reshape(64, 3, 3, 3, 64).transpose(1, 2, 3, 4, 0)).reshape(3, 768, 256)
+    w2 = banded(weight_two.reshape(64, 3, 3, 3, 64).transpose(1, 2, 3, 4, 0)).reshape(2304, 256)
     b1 = jnp.tile(bias_one, ACROSS)[None]
     b2 = jnp.tile(bias_two, ACROSS)[None]
 
-    made = compute_bricks(
-        count.reshape(1), cols, slots, flags, volume, zhalo, edge, w1, b1, w2, b2,
-        groups * capacity, columns,
-    )
-    arrived = lax.all_to_all(made, "xy", split_axis=0, concat_axis=0, tiled=True)
+    arrived = []
+    for begin, end in ((0, early), (early, columns)):
+        if begin < end:
+            amount, cols, slots, flags, part_capacity = part(begin, end)
+            made = compute_bricks(
+                amount, cols, slots, flags, volume, zhalo, edge, w1, b1, w2, b2,
+                groups * part_capacity, columns, end - begin,
+            )
+            sent = lax.all_to_all(made, "xy", split_axis=0, concat_axis=0, tiled=True)
+            arrived.append(sent.reshape(groups, part_capacity, 64, 512))
+    arrived = jnp.concatenate(arrived, axis=1).reshape(groups * capacity, 64, 512)
 
     my_label = jnp.sum(jnp.where(order == me, labels, 0))
     need = jnp.arange(slot_count, dtype=jnp.int32) * groups + my_label

time: 293 us -> 211 us (0.72)
  starting transfers between devices: 111 us -> 56.9 us
  Pallas kernels: 48 us -> 21.2 us
  waiting for transfers between devices: 29.6 us -> 20.5 us
    all_to_all x1 -> x2, starting transfers between devices: 100 us -> 49.3 us  [per_device(): sent = lax.all_to_all(made, 'xy', split_axis=0, concat_axis=0, tiled=True)]
    pallas_call x1 -> x2, Pallas kernels: 48 us -> 21.2 us  [compute_bricks(): pl.pallas_call(functools.partial(brick_kernel, columns=columns), out_shap...]
    all_to_all x1 -> x2, waiting for transfers between devices: 29.5 us -> 20.3 us  [per_device(): sent = lax.all_to_all(made, 'xy', split_axis=0, concat_axis=0, tiled=True)]
    ppermute x1, starting transfers between devices: 5.18 us -> 1.93 us  [per_device(): lax.ppermute(tail.reshape(layers, -1), 'xy', up_y).reshape(layers, 64, rims)]
  transfers between devices with their start and end apart: 5 -> 6, of which waited for: 1 -> 2; matrix products, arithmetic and copies ran while one was open for 7% -> 12% of each run, Pallas kernels for 0% -> 9%
where the time goes in v2:
time: 211 us; the launch traced here: 208 us
  blocking collectives  70.1 us (33%)
  starting transfers between devices  56.9 us (27%)
  Pallas kernels  21.2 us (10%)
  local copies, waits for them, and re-layouts  20.6 us (10%)
  waiting for transfers between devices  20.5 us (10%)
  other arithmetic  17.1 us (8%)
    all_gather x1, blocking collectives, per_device(): table = lax.all_gather(occupancy, ('gz', 'xy'), axis=0, tiled=True)  70.1 us
    all_to_all x2, starting transfers between devices, per_device(): sent = lax.all_to_all(made, 'xy', split_axis=0, concat_axis=0, tiled=True)  49.3 us
    pallas_call x2, Pallas kernels, compute_bricks(): pl.pallas_call(functools.partial(brick_kernel, columns=columns), out_shap...  21.2 us
    all_to_all x2, waiting for transfers between devices, per_device(): sent = lax.all_to_all(made, 'xy', split_axis=0, concat_axis=0, tiled=True)  20.3 us
  transfers between devices with their start and end apart: 6, of which 2 were waited for; matrix products, arithmetic and copies ran while one was open for 12% of the time, Pallas kernels for 9%

profile of v2, /device:TPU:0, one launch (start us, length us, event | category | flops | bytes accessed | tf_op | source)
XLA Modules:
  0.0 208.0 jit_solution(13850793849376522318)
XLA Ops:
  0.0 1.2 fusion.8
  1.2 3.1 %collective-permute-start = (bf16[1,64,2560]{2,1,0:T(8,128)(2,1)S(1)}, bf16[1,64,2560]{2,1,0:T(8,128)(2,1)}, u32[]{:S(2)}, u32[]{:S(2)}) collective-permute-start(bf16[1,64,2560]{2,1,0:T(8,128)(2,1)S(1)} %get-tuple-element.16), channel_id=1, source_target_pairs={{0,8},{8,16},{16,24},{1,9},{9,17},{17,25},{2,10},{10,18},{18,26},{... | collective-permute-start | bytes 983048 | tf_op jit(solution)/shard_map/ppermute | solution.py:224
  4.3 1.3 collective-permute-start.1
  5.6 2.3 %fusion.7 = (bf16[32,64,8]{2,1,0:T(8,128)(2,1)S(1)}, bf16[32,64,8]{2,1,0:T(8,128)(2,1)}) fusion(bf16[32,64,2560]{2,1,0:T(8,128)(2,1)} %next_ref.3), kind=kLoop, calls=%fused_computation.79 | loop fusion | bytes 131072 | tf_op jit(solution)/shard_map/slice | solution.py:229
  7.8 0.6 reduce_sum.142
  9.8 0.1 select_reduce_fusion.2
  9.9 70.1 %all-gather = s32[32,1,20]{2,1,0:T(1,128)S(1)} all-gather(s32[1,1,20]{2,1,0:T(1,128)S(1)} %bitcast.81), channel_id=1, replica_groups=mesh['gz'=4,'xy'=8] {'gz','xy'}, dimensions={0}, use_global_device_ids=true | all-gather | bytes 2640 | tf_op jit(solution)/shard_map/all_gather | solution.py:237
  80.0 0.5 broadcast.392
  80.5 0.7 reduce.7
  81.2 0.1 reshape.293
  81.3 1.2 fusion.6
  82.5 0.6 fusion
  83.2 0.7 and_select_fusion.3
  83.8 0.1 select_reduce_fusion.5
  83.9 0.1 pad_dynamic-slice_fusion
  84.1 0.1 copy.112
  84.3 0.3 reshape.302
  84.6 0.6 fusion.10
  85.3 0.2 copy.115
  85.4 0.2 copy.117
  85.6 0.2 copy.116
  85.8 0.7 select_reduce_fusion.8
  86.5 0.2 select_reduce_fusion.3
  86.8 0.2 select_reduce_fusion
  87.1 0.2 maximum_maximum_fusion.1
  87.3 3.2 %maximum_maximum_fusion = bf16[3,3,256,256]{3,2,1,0:T(8,128)(2,1)S(1)} fusion(bf16[3,3,64,64]{3,2,1,0:T(8,128)(2,1)S(1)} %bitcast.73, bf16[3,3,64,64]{3,2,1,0:T(8,128)(2,1)S(1)} %bitcast.74, bf16[3,3,64,128]{3,2,1,0:T(8,128)(2,1)S(1)} %broadcast.353, bf16[3,3,64,64]{3,2,1,0:T(8,128)(2,1)S(1)} %bitcast.75, bf16[3,3,64,64]{3,2,1,0:T(8,128)(2,1)S(1)} %broadcast_in_dim.197), kind=kLoop, calls=%fused_computation.2 | loop fusion | flops 16515072 | bytes 1622016 | tf_op jit(solution)/shard_map/concatenate | solution.py:45
  90.6 1.0 constant_dynamic-update-slice_fusion.1
  91.6 1.0 constant_dynamic-update-slice_fusion.zmain_ref.zprev_ref.znext_ref
  92.6 0.1 fusion.9
  92.7 2.1 pad_maximum_fusion.1
  94.8 1.8 copy.109
  96.5 1.9 collective-permute-start.3
  98.5 1.4 copy.108
  99.8 1.3 collective-permute-start.2
  101.1 0.9 select_reduce_fusion.1
  102.0 0.1 copy.118
  102.1 0.1 reshape.306.flags_ref
  102.2 0.7 tile.4
  102.8 0.1 broadcast_in_dim_tile.6.b1_ref
  102.9 0.7 tile.5
  103.6 0.1 broadcast_in_dim_tile.7.b2_ref
  103.7 0.1 copy.107
  103.8 0.1 reshape.295.flags_ref
  103.9 2.8 %copy.111 = bf16[34,64,8]{2,1,0:T(8,128)(2,1)} copy(bf16[34,64,8]{0,2,1:T(8,128)(2,1)} %bitcast.18) | data formatting | bytes 69632 | tf_op jit(solution)/shard_map/reshape | solution.py:231
  106.7 0.2 collective-permute-done.2
  106.9 1.8 copy.110
  108.8 1.6 pad_maximum_fusion.3.edge_ref
  110.3 2.7 %shard_map.110 = bf16[8,64,512]{2,1,0:T(8,128)(2,1)} custom-call(s32[1]{0:T(128)} %bitcast.32.n_ref, s32[4]{0:T(128)S(1)} %get-tuple-element.8.cols_ref, s32[4]{0:T(128)S(1)} %get-tuple-element.7.slots_ref, s32[36]{0:T(128)S(1)} %reshape.306.flags_ref, bf16[32,64,2560]{2,1,0:T(8,128)(2,1)} %next_ref.3, bf16[32,64,2560]{2,1,0:T(8,128)(2,1)} %next_ref.3, ...), custom_call_target="tpu_custom_call" | custom-call | flops 6400000000 | bytes 6400000 | tf_op jit(solution)/shard_map/pallas_call | solution.py:196
  113.0 10.4 %all-to-all-start.1 = ((bf16[8,64,512]{2,1,0:T(8,128)(2,1)}), bf16[8,64,512]{2,1,0:T(8,128)(2,1)}, u32[]{:S(2)}, u32[]{:S(2)}) async-start(bf16[8,64,512]{2,1,0:T(8,128)(2,1)} %shard_map.110), calls=%async_computation.1 | async-start | bytes 1048576 | tf_op jit(solution)/shard_map/all_to_all | solution.py:282
  123.5 18.5 %shard_map.109 = bf16[16,64,512]{2,1,0:T(8,128)(2,1)S(1)} custom-call(s32[1]{0:T(128)} %bitcast.2.n_ref, s32[16]{0:T(128)S(1)} %get-tuple-element.6.cols_ref, s32[16]{0:T(128)S(1)} %get-tuple-element.5.slots_ref, s32[144]{0:T(256)S(1)} %reshape.295.flags_ref, bf16[32,64,2560]{2,1,0:T(8,128)(2,1)} %next_ref.3, bf16[32,64,2560]{2,1,0:T(8,128)(2,1)} %next_ref.3, ...), custom_call_target="tpu_custom_call" | custom-call | flops 25600000000 | bytes 25600000 | tf_op jit(solution)/shard_map/pallas_call | solution.py:196
  142.0 1.0 copy-done
  143.0 38.8 %all-to-all-start = ((bf16[16,64,512]{2,1,0:T(8,128)(2,1)}), bf16[16,64,512]{2,1,0:T(8,128)(2,1)S(1)}, u32[]{:S(2)}, u32[]{:S(2)}) async-start(bf16[16,64,512]{2,1,0:T(8,128)(2,1)} %copy-done), calls=%async_computation | async-start | bytes 2097152 | tf_op jit(solution)/shard_map/all_to_all | solution.py:282
  181.9 0.1 reduce_sum.137
  182.0 0.1 select_reduce_fusion.7
  182.2 0.6 fusion.1
  182.8 0.6 multiply_add_fusion
  183.4 0.1 convert_reduce_fusion
  183.5 0.1 select_reduce_fusion.6
  183.6 0.7 fusion.3
  184.3 0.7 compare_and_fusion.2
  185.0 20.3 %all-to-all-done = bf16[16,64,512]{2,1,0:T(8,128)(2,1)S(1)} async-done(((bf16[16,64,512]{2,1,0:T(8,128)(2,1)}), bf16[16,64,512]{2,1,0:T(8,128)(2,1)S(1)}, u32[]{:S(2)}, u32[]{:S(2)}) %all-to-all-start) | async-done | bytes 1048608 | tf_op jit(solution)/shard_map/all_to_all | solution.py:282
  205.3 1.2 pad_maximum_fusion
  206.4 0.6 gather_fusion
  207.0 1.0 broadcast_select_fusion
  (37 shorter events, 0.4 us)
Async XLA Ops:
  0.0 7.8 %copy-start.6 = (s32[1,20]{1,0:T(1,128)S(1)}, s32[1,20]{1,0:T(1,128)}, u32[]{:S(2)}) copy-start(s32[1,20]{1,0:T(1,128)} %param.12) | copy-start | bytes 244
  0.0 83.8 %copy-start.7 = (s32[1,8]{1,0:T(1,128)S(1)}, s32[1,8]{1,0:T(1,128)}, u32[]{:S(2)}) copy-start(s32[1,8]{1,0:T(1,128)} %param.13) | copy-start | bytes 100
  0.0 84.1 %copy-start.4 = (bf16[64,576]{1,0:T(8,128)(2,1)S(1)}, bf16[64,576]{1,0:T(8,128)(2,1)}, u32[]{:S(2)}) copy-start(bf16[64,576]{1,0:T(8,128)(2,1)} %param.14) | copy-start | bytes 221188
  0.0 84.3 %copy-start.3 = (bf16[64,1728]{1,0:T(8,128)(2,1)S(1)}, bf16[64,1728]{1,0:T(8,128)(2,1)}, u32[]{:S(2)}) copy-start(bf16[64,1728]{1,0:T(8,128)(2,1)} %param.16) | copy-start | bytes 663556
  1.2 89.4 %collective-permute-start = (bf16[1,64,2560]{2,1,0:T(8,128)(2,1)S(1)}, bf16[1,64,2560]{2,1,0:T(8,128)(2,1)}, u32[]{:S(2)}, u32[]{:S(2)}) collective-permute-start(bf16[1,64,2560]{2,1,0:T(8,128)(2,1)S(1)} %get-tuple-element.16), channel_id=1, source_target_pairs={{0,8},{8,16},{16,24},{1,9},{9,17},{17,25},{2,10},{10,18},{18,26},{... | collective-permute-start | bytes 983048 | tf_op jit(solution)/shard_map/ppermute | solution.py:224
  4.3 87.3 %collective-permute-start.1 = (bf16[1,64,2560]{2,1,0:T(8,128)(2,1)S(1)}, bf16[1,64,2560]{2,1,0:T(8,128)(2,1)}, u32[]{:S(2)}, u32[]{:S(2)}) collective-permute-start(bf16[1,64,2560]{2,1,0:T(8,128)(2,1)S(1)} %get-tuple-element.15), channel_id=1, source_target_pairs={{8,0},{16,8},{24,16},{9,1},{17,9},{25,17},{10,2},{18,10},{26,18},{... | collective-permute-start | bytes 983048 | tf_op jit(solution)/shard_map/ppermute | solution.py:225
  94.8 15.6 %copy-start.1 = (bf16[2,256,512]{2,1,0:T(8,128)(2,1)S(1)}, bf16[2,256,512]{2,1,0:T(8,128)(2,1)}, u32[]{:S(2)}) copy-start(bf16[2,256,512]{2,1,0:T(8,128)(2,1)} %constant.102.clone.inter_ref) | copy-start | bytes 1572868
  94.8 15.6 %copy-start.2 = (bf16[160,256]{1,0:T(8,128)(2,1)S(1)}, bf16[160,256]{1,0:T(8,128)(2,1)}, u32[]{:S(2)}) copy-start(bf16[160,256]{1,0:T(8,128)(2,1)} %constant.101.clone.spread_ref) | copy-start | bytes 245764
  96.5 7.4 %collective-permute-start.3 = (bf16[34,512]{0,1:T(8,128)(2,1)S(1)}, bf16[34,512]{0,1:T(8,128)(2,1)}, u32[]{:S(2)}, u32[]{:S(2)}) collective-permute-start(bf16[34,512]{0,1:T(8,128)(2,1)S(1)} %bitcast.76), channel_id=1, source_target_pairs={{0,1},{1,2},{2,3},{3,4},{4,5},{5,6},{6,7},{8,9},{9,10},{10,11},{11... | collective-permute-start | bytes 104456 | tf_op jit(solution)/shard_map/ppermute | solution.py:231
  99.8 7.1 %collective-permute-start.2 = (bf16[34,512]{0,1:T(8,128)(2,1)}, bf16[34,512]{0,1:T(8,128)(2,1)S(1)}, u32[]{:S(2)}, u32[]{:S(2)}) collective-permute-start(bf16[34,512]{0,1:T(8,128)(2,1)} %bitcast.77), channel_id=1, source_target_pairs={{1,0},{2,1},{3,2},{4,3},{5,4},{6,5},{7,6},{9,8},{10,9},{11,10},{12... | collective-permute-start | bytes 104456 | tf_op jit(solution)/shard_map/ppermute | solution.py:232
  113.0 29.9 %all-to-all-start.1 = ((bf16[8,64,512]{2,1,0:T(8,128)(2,1)}), bf16[8,64,512]{2,1,0:T(8,128)(2,1)}, u32[]{:S(2)}, u32[]{:S(2)}) async-start(bf16[8,64,512]{2,1,0:T(8,128)(2,1)} %shard_map.110), calls=%async_computation.1 | async-start | bytes 1048576 | tf_op jit(solution)/shard_map/all_to_all | solution.py:282
  123.4 58.4 %copy-start.5 = (s32[160]{0:T(256)S(1)}, s32[160]{0:T(256)}, u32[]{:S(2)}) copy-start(s32[160]{0:T(256)} %get-tuple-element.9) | copy-start | bytes 1924
  123.4 58.7 %copy-start.8 = (s32[1,8]{1,0:T(1,128)S(1)}, s32[1,8]{1,0:T(1,128)}, u32[]{:S(2)}) copy-start(s32[1,8]{1,0:T(1,128)} %param.13) | copy-start | bytes 100
  142.0 1.0 copy-start
  143.0 62.3 %all-to-all-start = ((bf16[16,64,512]{2,1,0:T(8,128)(2,1)}), bf16[16,64,512]{2,1,0:T(8,128)(2,1)S(1)}, u32[]{:S(2)}, u32[]{:S(2)}) async-start(bf16[16,64,512]{2,1,0:T(8,128)(2,1)} %copy-done), calls=%async_computation | async-start | bytes 2097152 | tf_op jit(solution)/shard_map/all_to_all | solution.py:282

commit v3 on v2

--- a/solution.py
+++ b/solution.py
@@ -68,10 +68,12 @@
         low = lane < 64
         from_edge = jnp.where(low, last.astype(jnp.int32), first.astype(jnp.int32)) > 0
 
+        def keep(value, mark):
+            return jnp.where(mark > 0, value, jnp.zeros((), BF))
+
         def rim(before, after, edge, a):
             value = jnp.where(from_edge, edge, jnp.where(low, after, before))
-            mask = jnp.where(low, flag(a, 2), flag(a, 0)).astype(BF)
-            return value * mask
+            return keep(value, jnp.where(low, flag(a, 2), flag(a, 0)))
 
         spread = spread_ref[...]
 
@@ -100,7 +102,7 @@
         def put_rim(layer, a, spot):
             at = slice(layer, layer + 1)
             side = rim(zprev_ref[at], znext_ref[at], edge_ref[32 + layer:33 + layer], a)
-            put(zmain_ref[at] * flag(a, 1).astype(BF), side, spot)
+            put(keep(zmain_ref[at], flag(a, 1)), side, spot)
 
         y_at = lax.broadcasted_iota(jnp.int32, (PITCH, 256), 0)
         regions = [
@@ -207,39 +209,177 @@
       spread, inter, w1, b1, w2, b2)
 
 
+MESH = pl.DeviceIdType.MESH
+
+
+def exchange_kernel(
+    volume_ref, occ_ref, zhalo_ref, edge_ref, table_ref, near_ref,
+    head_ref, tail_ref, packed_ref, landed_ref, corner_ref, occ_out_ref,
+    local_sem, occ_send, occ_recv, near_send, near_recv, rim_send, rim_recv,
+    *, slabs, groups, columns,
+):
+    gz = lax.axis_index("gz")
+    xy = lax.axis_index("xy")
+    span = volume_ref.shape[2]
+
+    def exists(dz, dy):
+        return (gz + dz >= 0) & (gz + dz < slabs) & (xy + dy >= 0) & (xy + dy < groups)
+
+    around = [(dz, dy) for dz in (-1, 0, 1) for dy in (-1, 0, 1) if (dz, dy) != (0, 0)]
+    local = [
+        pltpu.make_async_copy(volume_ref.at[:, :, pl.ds(0, 128)], head_ref, local_sem.at[0]),
+        pltpu.make_async_copy(
+            volume_ref.at[:, :, pl.ds(span - 128, 128)], tail_ref, local_sem.at[1]
+        ),
+    ]
+    for copy in local:
+        copy.start()
+
+    occ_out_ref[...] = jnp.zeros((8, 128), jnp.int32)
+    occ_out_ref[0:1, 0:columns] = occ_ref[...]
+    near_ref[...] = jnp.zeros((3, 3, 8, 128), jnp.int32)
+    near_ref[1, 1] = occ_out_ref[...]
+    landed_ref[...] = jnp.zeros_like(landed_ref)
+    corner_ref[...] = jnp.zeros_like(corner_ref)
+    table_ref[xy] = occ_out_ref[...]
+
+    barrier = pltpu.get_barrier_semaphore()
+    partners = groups - 1
+    for step in range(1, groups):
+        pl.semaphore_signal(
+            barrier, inc=1, device_id=(gz, lax.rem(xy + step, groups)), device_id_type=MESH
+        )
+    for dz, dy in around:
+        if dz != 0:
+            partners = partners + exists(dz, dy).astype(jnp.int32)
+
+            @pl.when(exists(dz, dy))
+            def _(dz=dz, dy=dy):
+                pl.semaphore_signal(
+                    barrier, inc=1, device_id=(gz + dz, xy + dy), device_id_type=MESH
+                )
+
+    pl.semaphore_wait(barrier, partners)
+
+    marks = []
+    for step in range(1, groups):
+        marks.append(pltpu.make_async_remote_copy(
+            src_ref=occ_out_ref, dst_ref=table_ref.at[xy],
+            send_sem=occ_send.at[step], recv_sem=occ_recv.at[step],
+            device_id=(gz, lax.rem(xy + step, groups)), device_id_type=MESH,
+        ))
+        marks[-1].start()
+
+    guarded = []
+
+    def send(dz, dy, src, dst, send_sem, recv_sem):
+        copy = pltpu.make_async_remote_copy(
+            src_ref=src, dst_ref=dst, send_sem=send_sem, recv_sem=recv_sem,
+            device_id=(gz + dz, xy + dy), device_id_type=MESH,
+        )
+        pl.when(exists(dz, dy))(copy.start)
+        guarded.append((dz, dy, copy))
+
+    send(1, 0, volume_ref.at[SIDE - 1], zhalo_ref.at[0], rim_send.at[0], rim_recv.at[0])
+    send(-1, 0, volume_ref.at[0], zhalo_ref.at[1], rim_send.at[1], rim_recv.at[1])
+    for k, (dz, dy) in enumerate(around):
+        send(
+            dz, dy, occ_out_ref, near_ref.at[1 - dz, 1 - dy], near_send.at[k], near_recv.at[k]
+        )
+    for copy in local:
+        copy.wait()
+    corners = (
+        (1, 1, tail_ref, SIDE - 1), (1, -1, head_ref, SIDE - 1),
+        (-1, 1, tail_ref, 0), (-1, -1, head_ref, 0),
+    )
+    for k, (dz, dy, source, layer) in enumerate(corners):
+        send(dz, dy, source.at[layer], corner_ref.at[k], rim_send.at[2 + k], rim_recv.at[2 + k])
+
+    lane = lax.broadcasted_iota(jnp.int32, (1, 128), 1)
+    for which, source, origin in ((0, tail_ref, 120), (1, head_ref, 0)):
+        for group in range(2):
+            packed = jnp.zeros((64, 128), F32)
+            for k in range(16):
+                value = source[group * 16 + k].astype(F32)
+                shift = (8 * k - origin) % 128
+                value = pltpu.roll(value, shift, 1) if shift else value
+                packed = jnp.where((lane >= 8 * k) & (lane < 8 * k + 8), value, packed)
+            packed_ref[which, group] = packed.astype(BF)
+    for which, dy in ((0, 1), (1, -1)):
+        send(
+            0, dy, packed_ref.at[which], landed_ref.at[which],
+            rim_send.at[6 + which], rim_recv.at[6 + which],
+        )
+
+    for dz, dy, copy in guarded:
+        pl.when(exists(-dz, -dy))(copy.wait_recv)
+    for copy in marks:
+        copy.wait_recv()
+
+    zero = jnp.zeros((64, 128), F32)
+    for group in range(2):
+        before = landed_ref[0, group].astype(F32)
+        after = landed_ref[1, group].astype(F32)
+        for k in range(16):
+            up = (120 - 8 * k) % 128
+            down = (-8 * k) % 128
+            left = pltpu.roll(before, up, 1) if up else before
+            right = pltpu.roll(after, down, 1) if down else after
+            value = jnp.where(lane < 8, right, jnp.where(lane >= 120, left, zero))
+            edge_ref[group * 16 + k] = value.astype(BF)
+    for layer in range(2):
+        left = corner_ref[2 * layer].astype(F32)
+        right = corner_ref[2 * layer + 1].astype(F32)
+        value = jnp.where(lane < 8, right, jnp.where(lane >= 120, left, zero))
+        edge_ref[SIDE + layer] = value.astype(BF)
+
+    for dz, dy, copy in guarded:
+        pl.when(exists(dz, dy))(copy.wait_send)
+    for copy in marks:
+        copy.wait_send()
+
+
+def exchange(volume, occupancy, slabs, groups, columns):
+    vmem = pl.BlockSpec(memory_space=pltpu.VMEM)
+    anywhere = pl.BlockSpec(memory_space=pl.ANY)
+    dma = pltpu.SemaphoreType.DMA
+    return pl.pallas_call(
+        functools.partial(exchange_kernel, slabs=slabs, groups=groups, columns=columns),
+        out_shape=(
+            jax.ShapeDtypeStruct((2,) + volume.shape[1:], BF),
+            jax.ShapeDtypeStruct((SIDE + 2, 64, 128), BF),
+            jax.ShapeDtypeStruct((groups, 8, 128), jnp.int32),
+            jax.ShapeDtypeStruct((3, 3, 8, 128), jnp.int32),
+        ),
+        in_specs=[anywhere, vmem],
+        out_specs=(anywhere, vmem, vmem, vmem),
+        scratch_shapes=[
+            pltpu.VMEM((SIDE, 64, 128), BF),
+            pltpu.VMEM((SIDE, 64, 128), BF),
+            pltpu.VMEM((2, 2, 64, 128), BF),
+            pltpu.VMEM((2, 2, 64, 128), BF),
+            pltpu.VMEM((4, 64, 128), BF),
+            pltpu.VMEM((8, 128), jnp.int32),
+            dma((2,)), dma((groups,)), dma((groups,)), dma((8,)), dma((8,)), dma((8,)), dma((8,)),
+        ],
+        compiler_params=pltpu.CompilerParams(
+            collective_id=0, has_side_effects=True, vmem_limit_bytes=16 * 1024 * 1024
+        ),
+        cost_estimate=pl.CostEstimate(flops=0, bytes_accessed=2_000_000, transcendentals=0),
+    )(volume, occupancy)
+
+
 def per_device(volume, occupancy, device_order, weight_one, bias_one, weight_two, bias_two):
     columns = occupancy.shape[1]
     slabs = lax.axis_size("gz")
     groups = lax.axis_size("xy")
     capacity = (columns + groups - 1) // groups
     slot_count = columns // 2
-    me_z = lax.axis_index("gz")
     me = lax.axis_index("xy")
-    rims = 2 * ACROSS
-
-    up_z = [(i, i + 1) for i in range(slabs - 1)]
-    down_z = [(j, i) for i, j in up_z]
-    up_y = [(i, i + 1) for i in range(groups - 1)]
-    down_y = [(j, i) for i, j in up_y]
-    below = lax.ppermute(volume[SIDE - 1:], "gz", up_z)
-    above = lax.ppermute(volume[:1], "gz", down_z)
-    zhalo = jnp.concatenate([below, above], axis=0)
-    span = volume.shape[2]
-    tail = jnp.concatenate([volume[:, :, span - rims:], zhalo[:, :, span - rims:]], axis=0)
-    head = jnp.concatenate([volume[:, :, :rims], zhalo[:, :, :rims]], axis=0)
-    layers = tail.shape[0]
-    before = lax.ppermute(tail.reshape(layers, -1), "xy", up_y).reshape(layers, 64, rims)
-    after = lax.ppermute(head.reshape(layers, -1), "xy", down_y).reshape(layers, 64, rims)
-    edge = jnp.concatenate(
-        [after, jnp.zeros((layers, 64, 128 - 2 * rims), BF), before], axis=2
-    )
-
-    table = lax.all_gather(occupancy, ("gz", "xy"), axis=0, tiled=True)
-    table = table.reshape(slabs, groups * columns)
+    zhalo, edge, table, near = exchange(volume, occupancy, slabs, groups, columns)
     total = groups * columns
-    marks = jnp.pad(table, ((1, 1), (1, 1)))
-    near = lax.dynamic_slice(marks, (me_z, me * columns), (3, columns + 2))
-    row = lax.dynamic_slice(table, (me_z, 0), (1, total))[0]
+    row = table[:, 0, :columns].reshape(total)
+    near = near[:, :, 0, :columns].reshape(3, 3 * columns)[:, columns - 1:2 * columns + 1]
     own = occupancy[0]
     order = device_order[0]
     ids = jnp.arange(columns, dtype=jnp.int32)

time: 211 us -> 138 us (0.65); the launches traced: 208 us -> 139 us
  blocking collectives: 70.1 us -> 0 us
  Pallas kernels: 21.2 us -> 78.8 us
  starting transfers between devices: 56.9 us -> 10 us
  local copies, waits for them, and re-layouts: 20.6 us -> 9.62 us
  waiting for transfers between devices: 20.5 us -> 24.3 us
  other arithmetic: 17.1 us -> 14.9 us
    all_gather x1 -> x0, blocking collectives: 70.1 us -> none  [per_device(): table = lax.all_gather(occupancy, ('gz', 'xy'), axis=0, tiled=True)]
    pallas_call x2, Pallas kernels: 21.2 us -> 68.8 us  [compute_bricks(): pl.pallas_call(functools.partial(brick_kernel, columns=columns), out_shap...]
    all_to_all x2, starting transfers between devices: 49.3 us -> 10 us  [per_device(): sent = lax.all_to_all(made, 'xy', split_axis=0, concat_axis=0, tiled=True)]
    pallas_call x0 -> x1, Pallas kernels: none -> 9.98 us  [exchange(): pl.pallas_call(functools.partial(exchange_kernel, slabs=slabs, groups=gro...]
    ppermute x4 -> x0, starting transfers between devices: 7.6 us -> none  [the longest x1 3.11 us: per_device(): below = lax.ppermute(volume[SIDE - 1:], 'gz', up_z)]
    reshape x3 -> x0, local copies, waits for them, and re-layouts: 4.68 us -> none  [the longest x1 2.75 us: per_device(): lax.ppermute(tail.reshape(layers, -1), 'xy', up_y).reshape(layers, 64, rims)]
    concatenate x4 -> x0, local copies, waits for them, and re-layouts: 4.24 us -> none  [the longest x1 1.78 us: per_device(): jnp.concatenate([volume[:, :, span - rims:], zhalo[:, :, span - rims:]],...]
    all_to_all x2, waiting for transfers between devices: 20.3 us -> 24.3 us  [per_device(): sent = lax.all_to_all(made, 'xy', split_axis=0, concat_axis=0, tiled=True)]
  transfers between devices with their start and end apart: 6 -> 2, of which waited for: 2 -> 1; matrix products, arithmetic and copies ran while one was open for 12% -> 3% of each run, Pallas kernels for 9% -> 39%
where the time goes in v3:
time: 138 us; the launch traced here: 139 us
  Pallas kernels  78.8 us (57%)
  waiting for transfers between devices  24.3 us (18%)
  other arithmetic  14.9 us (11%)
  starting transfers between devices  10 us (7%)
  local copies, waits for them, and re-layouts  9.62 us (7%)
    pallas_call x2, Pallas kernels, compute_bricks(): pl.pallas_call(functools.partial(brick_kernel, columns=columns), out_shap...  68.8 us
    all_to_all x2, waiting for transfers between devices, per_device(): sent = lax.all_to_all(made, 'xy', split_axis=0, concat_axis=0, tiled=True)  24.3 us
    all_to_all x2, starting transfers between devices, per_device(): sent = lax.all_to_all(made, 'xy', split_axis=0, concat_axis=0, tiled=True)  10 us
    pallas_call x1, Pallas kernels, exchange(): pl.pallas_call(functools.partial(exchange_kernel, slabs=slabs, groups=gro...  9.98 us
    unnamed x19, local copies, waits for them, and re-layouts  4.82 us
    concatenate x2, other arithmetic, banded(): return jnp.concatenate(rows, axis=-2)  4.72 us
    slice x4, local copies, waits for them, and re-layouts, banded(): blocks.append(taps[..., tap, :, :] if 0 <= tap < 3 else zero)  3.04 us
  transfers between devices with their start and end apart: 2, of which 1 were waited for; matrix products, arithmetic and copies ran while one was open for 3% of the time, Pallas kernels for 39%

profile of v3, /device:TPU:0, one launch (start us, length us, event | category | flops | bytes accessed | tf_op | source)
XLA Modules:
  0.0 139.0 jit_solution(9849484216309883390)
XLA Ops:
  0.0 0.7 compare_bitcast_fusion
  0.7 1.3 reduce_sum.142
  2.5 0.8 select_reduce_fusion.2
  3.2 0.0 copy-start
  3.3 4.0 %copy-done = bf16[32,64,2560]{2,1,0:T(8,128)(2,1)S(1)} copy-done((bf16[32,64,2560]{2,1,0:T(8,128)(2,1)S(1)}, bf16[32,64,2560]{2,1,0:T(8,128)(2,1)}, u32[]{:S(2)}) %copy-start) | copy-done | bytes 10485784
  7.2 0.0 copy-start.3
  7.2 0.7 copy-done.3
  7.9 0.0 copy-start.8
  7.9 0.0 copy-start.5
  7.9 0.0 copy-start.6
  7.9 0.0 copy-start.4
  7.9 10.0 %shard_map.109 = (bf16[2,64,2560]{2,1,0:T(8,128)(2,1)S(1)}, bf16[34,64,128]{2,1,0:T(8,128)(2,1)S(1)}, s32[8,8,128]{2,1,0:T(8,128)S(1)}, s32[3,3,8,128]{3,2,1,0:T(8,128)S(1)}) custom-call(bf16[32,64,2560]{2,1,0:T(8,128)(2,1)S(1)} %copy-done, s32[1,20]{1,0:T(1,128)S(1)} %copy-done.3), custom_call_target="tpu_custom_call" | custom-call | bytes 2000000 | tf_op jit(solution)/shard_map/pallas_call | solution.py:346
  17.9 0.0 copy-start.7
  17.9 0.8 slice_reduce_fusion.1
  18.7 0.7 and_select_fusion.3
  19.3 0.0 copy-done.8
  19.4 0.1 select_reduce_fusion.5
  19.5 0.1 reshape_squeeze.4
  19.6 0.1 slice_bitcast_fusion.3
  19.7 0.2 select_reduce_fusion.8
  19.9 0.2 select_reduce_fusion.1
  20.1 0.1 copy.77
  20.2 0.1 reshape.302.flags_ref
  20.3 0.0 copy-done.5
  20.3 0.2 copy.71
  20.5 0.0 copy-done.6
  20.5 0.1 broadcast_in_dim_tile.6.b1_ref
  20.6 0.0 copy-done.4
  20.6 0.3 reshape.298
  20.9 0.6 fusion.6
  21.6 0.0 copy-start.1
  21.6 0.0 copy-start.2
  21.6 0.8 copy.74
  22.4 0.8 copy.76
  23.2 0.8 copy.75
  24.0 0.0 copy-done.7
  24.0 0.1 broadcast_in_dim_tile.7.b2_ref
  24.1 0.2 maximum_maximum_fusion.1
  24.4 4.5 %maximum_maximum_fusion = bf16[3,3,256,256]{3,2,1,0:T(8,128)(2,1)S(1)} fusion(bf16[3,3,64,64]{3,2,1,0:T(8,128)(2,1)} %bitcast.68, bf16[3,3,64,64]{3,2,1,0:T(8,128)(2,1)} %bitcast.69, bf16[3,3,64,128]{3,2,1,0:T(8,128)(2,1)S(1)} %broadcast.372, bf16[3,3,64,64]{3,2,1,0:T(8,128)(2,1)} %bitcast.70, bf16[3,3,64,64]{3,2,1,0:T(8,128)(2,1)S(1)} %broadcast_in_dim.193), kind=kLoop, calls=%fused_computation.2 | loop fusion | flops 16515072 | bytes 1622016 | tf_op jit(solution)/shard_map/concatenate | solution.py:45
  28.9 0.0 copy-done.1
  28.9 0.0 copy-done.2
  28.9 15.2 %shard_map.111 = bf16[8,64,512]{2,1,0:T(8,128)(2,1)} custom-call(s32[1]{0:T(128)} %bitcast.26.n_ref, s32[4]{0:T(128)S(1)} %get-tuple-element.18.cols_ref, s32[4]{0:T(128)S(1)} %get-tuple-element.17.slots_ref, s32[36]{0:T(128)S(1)} %reshape.302.flags_ref, bf16[32,64,2560]{2,1,0:T(8,128)(2,1)} %next_ref.3, bf16[32,64,2560]{2,1,0:T(8,128)(2,1)} %next_ref.3, ...), custom_call_target="tpu_custom_call" | custom-call | flops 6400000000 | bytes 6400000 | tf_op jit(solution)/shard_map/pallas_call | solution.py:198
  44.2 4.1 %all-to-all-start.1 = ((bf16[8,64,512]{2,1,0:T(8,128)(2,1)}), bf16[8,64,512]{2,1,0:T(8,128)(2,1)}, u32[]{:S(2)}, u32[]{:S(2)}) async-start(bf16[8,64,512]{2,1,0:T(8,128)(2,1)} %shard_map.111), calls=%async_computation.1 | async-start | bytes 1048576 | tf_op jit(solution)/shard_map/all_to_all | solution.py:422
  48.9 0.2 select_reduce_fusion.3
  49.1 0.2 select_reduce_fusion
  49.3 0.1 copy.70
  49.4 0.1 reshape.295.flags_ref
  49.5 53.6 %shard_map.110 = bf16[16,64,512]{2,1,0:T(8,128)(2,1)} custom-call(s32[1]{0:T(128)} %bitcast.1.n_ref, s32[16]{0:T(128)S(1)} %get-tuple-element.16.cols_ref, s32[16]{0:T(128)S(1)} %get-tuple-element.15.slots_ref, s32[144]{0:T(256)S(1)} %reshape.295.flags_ref, bf16[32,64,2560]{2,1,0:T(8,128)(2,1)} %next_ref.3, bf16[32,64,2560]{2,1,0:T(8,128)(2,1)} %next_ref.3, ...), custom_call_target="tpu_custom_call" | custom-call | flops 25600000000 | bytes 25600000 | tf_op jit(solution)/shard_map/pallas_call | solution.py:198
  103.1 0.0 all-to-all-done.1
  103.1 5.9 %all-to-all-start = ((bf16[16,64,512]{2,1,0:T(8,128)(2,1)}), bf16[16,64,512]{2,1,0:T(8,128)(2,1)S(1)}, u32[]{:S(2)}, u32[]{:S(2)}) async-start(bf16[16,64,512]{2,1,0:T(8,128)(2,1)} %shard_map.110), calls=%async_computation | async-start | bytes 2097152 | tf_op jit(solution)/shard_map/all_to_all | solution.py:422
  109.0 0.1 select_reduce_fusion.7
  109.1 0.6 fusion.1
  109.7 0.6 multiply_add_fusion
  110.4 0.1 convert_reduce_fusion
  110.5 0.1 select_reduce_fusion.6
  110.6 0.7 fusion.3
  111.2 0.7 compare_and_fusion.2
  111.9 24.3 %all-to-all-done = bf16[16,64,512]{2,1,0:T(8,128)(2,1)S(1)} async-done(((bf16[16,64,512]{2,1,0:T(8,128)(2,1)}), bf16[16,64,512]{2,1,0:T(8,128)(2,1)S(1)}, u32[]{:S(2)}, u32[]{:S(2)}) %all-to-all-start) | async-done | bytes 1048608 | tf_op jit(solution)/shard_map/all_to_all | solution.py:422
  136.2 1.2 pad_maximum_fusion
  137.4 0.6 gather_fusion
  138.0 1.0 broadcast_select_fusion
  (14 shorter events, 0.2 us)
Async XLA Ops:
  3.2 4.0 %copy-start = (bf16[32,64,2560]{2,1,0:T(8,128)(2,1)S(1)}, bf16[32,64,2560]{2,1,0:T(8,128)(2,1)}, u32[]{:S(2)}) copy-start(bf16[32,64,2560]{2,1,0:T(8,128)(2,1)} %next_ref.3) | copy-start | bytes 31457284
  7.2 0.7 copy-start.3
  7.9 11.5 %copy-start.8 = (s32[1,8]{1,0:T(1,128)S(1)}, s32[1,8]{1,0:T(1,128)}, u32[]{:S(2)}) copy-start(s32[1,8]{1,0:T(1,128)} %param.13) | copy-start | bytes 100
  7.9 12.4 %copy-start.5 = (bf16[64,576]{1,0:T(8,128)(2,1)S(1)}, bf16[64,576]{1,0:T(8,128)(2,1)}, u32[]{:S(2)}) copy-start(bf16[64,576]{1,0:T(8,128)(2,1)} %param.14) | copy-start | bytes 221188
  7.9 12.6 %copy-start.6 = (f32[64]{0:T(128)S(1)}, f32[64]{0:T(128)}, u32[]{:S(2)}) copy-start(f32[64]{0:T(128)} %param.15) | copy-start | bytes 772
  7.9 12.7 %copy-start.4 = (bf16[64,1728]{1,0:T(8,128)(2,1)S(1)}, bf16[64,1728]{1,0:T(8,128)(2,1)}, u32[]{:S(2)}) copy-start(bf16[64,1728]{1,0:T(8,128)(2,1)} %param.16) | copy-start | bytes 663556
  17.9 6.1 %copy-start.7 = (f32[64]{0:T(128)S(1)}, f32[64]{0:T(128)}, u32[]{:S(2)}) copy-start(f32[64]{0:T(128)} %param.17) | copy-start | bytes 772
  21.6 7.3 %copy-start.1 = (bf16[2,256,512]{2,1,0:T(8,128)(2,1)S(1)}, bf16[2,256,512]{2,1,0:T(8,128)(2,1)}, u32[]{:S(2)}) copy-start(bf16[2,256,512]{2,1,0:T(8,128)(2,1)} %constant.96.clone.inter_ref) | copy-start | bytes 1572868
  21.6 7.3 %copy-start.2 = (bf16[160,256]{1,0:T(8,128)(2,1)S(1)}, bf16[160,256]{1,0:T(8,128)(2,1)}, u32[]{:S(2)}) copy-start(bf16[160,256]{1,0:T(8,128)(2,1)} %constant.95.clone.spread_ref) | copy-start | bytes 245764
  44.2 58.9 %all-to-all-start.1 = ((bf16[8,64,512]{2,1,0:T(8,128)(2,1)}), bf16[8,64,512]{2,1,0:T(8,128)(2,1)}, u32[]{:S(2)}, u32[]{:S(2)}) async-start(bf16[8,64,512]{2,1,0:T(8,128)(2,1)} %shard_map.111), calls=%async_computation.1 | async-start | bytes 1048576 | tf_op jit(solution)/shard_map/all_to_all | solution.py:422
  103.1 33.1 %all-to-all-start = ((bf16[16,64,512]{2,1,0:T(8,128)(2,1)}), bf16[16,64,512]{2,1,0:T(8,128)(2,1)S(1)}, u32[]{:S(2)}, u32[]{:S(2)}) async-start(bf16[16,64,512]{2,1,0:T(8,128)(2,1)} %shard_map.110), calls=%async_computation | async-start | bytes 2097152 | tf_op jit(solution)/shard_map/all_to_all | solution.py:422

commit v4 on v3

--- a/solution.py
+++ b/solution.py
@@ -33,27 +33,129 @@
     return table
 
 
-def banded(taps):
-    zero = jnp.zeros_like(taps[..., 0, :, :])
-    rows = []
-    for xi in range(ACROSS):
-        blocks = []
-        for xo in range(ACROSS):
-            tap = xi - xo + 1
-            blocks.append(taps[..., tap, :, :] if 0 <= tap < 3 else zero)
-        rows.append(jnp.concatenate(blocks, axis=-1))
-    return jnp.concatenate(rows, axis=-2)
+def plan_kernel(
+    table_ref, near_ref, order_ref, w1_ref, b1_ref, w2_ref, b2_ref,
+    count_ref, cols_ref, slots_ref, flags_ref, owner_ref, part_ref,
+    band1_ref, wide1_ref, band2_ref, wide2_ref, start_ref,
+    *, groups, columns,
+):
+    xy = lax.axis_index("xy")
+
+    def tally(g, before):
+        start_ref[g] = before
+        return lax.fori_loop(0, columns, lambda j, t: t + table_ref[g, 0, j], before)
+
+    start_ref[groups] = lax.fori_loop(0, groups, tally, jnp.int32(0))
+    first = start_ref[xy]
+
+    def place(j, rank):
+        label = lax.rem(first + rank, groups)
+        cols_ref[rank] = j
+        slots_ref[rank] = order_ref[0, label]
+        for b in range(3):
+            at = j + b - 1
+            block = jnp.where(at < 0, 0, jnp.where(at >= columns, 2, 1))
+            spot = jnp.where(at < 0, columns - 1, jnp.where(at >= columns, 0, at))
+            for a in range(3):
+                flags_ref[rank * 9 + 3 * a + b] = near_ref[a, block, 0, spot]
+        return rank + table_ref[xy, 0, j]
+
+    slots_ref[0] = 0
+    count = lax.fori_loop(0, columns, place, jnp.int32(0))
+    count_ref[0] = count
+    last = jnp.maximum(count - 1, 0)
+
+    def repeat(i, carry):
+        cols_ref[i] = cols_ref[last]
+        slots_ref[i] = slots_ref[last]
+        return carry
+
+    lax.fori_loop(count, columns, repeat, 0)
+
+    mine = lax.fori_loop(
+        0, groups, lambda g, t: jnp.where(order_ref[0, g] == xy, g, t), jnp.int32(0)
+    )
+
+    def arrive(k, carry):
+        need = k * groups + mine
+        owner = lax.fori_loop(
+            1, groups, lambda g, t: t + (start_ref[g] <= need).astype(jnp.int32), jnp.int32(0)
+        )
+        owner_ref[k] = owner
+        part_ref[k] = (need - start_ref[owner]) // groups
+        return carry
+
+    lax.fori_loop(0, columns // 2, arrive, 0)
+
+    zero = jnp.zeros((64, 64), BF)
+    for source, band in ((w1_ref, band1_ref), (w2_ref, band2_ref)):
+        for row in range(source.shape[0] // 192):
+            taps = [source[(3 * row + t) * 64:(3 * row + t + 1) * 64, :] for t in range(3)]
+            for xi in range(ACROSS):
+                blocks = [
+                    taps[xi - xo + 1] if 0 <= xi - xo + 1 < 3 else zero for xo in range(ACROSS)
+                ]
+                at = (ACROSS * row + xi) * 64
+                band[at:at + 64, :] = jnp.concatenate(blocks, axis=1)
+    wide1_ref[...] = jnp.concatenate([b1_ref[...]] * ACROSS, axis=1)
+    wide2_ref[...] = jnp.concatenate([b2_ref[...]] * ACROSS, axis=1)
+
+
+def plan(table, near, order, weight_one, bias_one, weight_two, bias_two, groups, columns):
+    vmem = pl.BlockSpec(memory_space=pltpu.VMEM)
+    smem = pl.BlockSpec(memory_space=pltpu.SMEM)
+
+    def ints(length):
+        return jax.ShapeDtypeStruct((length,), jnp.int32)
+
+    return pl.pallas_call(
+        functools.partial(plan_kernel, groups=groups, columns=columns),
+        out_shape=(
+            ints(1), ints(columns + 1), ints(columns + 1), ints(9 * columns + 9),
+            ints(columns // 2), ints(columns // 2),
+            jax.ShapeDtypeStruct((768, 256), BF), jax.ShapeDtypeStruct((1, 256), F32),
+            jax.ShapeDtypeStruct((2304, 256), BF), jax.ShapeDtypeStruct((1, 256), F32),
+        ),
+        in_specs=[smem] * 3 + [vmem] * 4,
+        out_specs=(smem,) * 6 + (vmem,) * 4,
+        scratch_shapes=[pltpu.SMEM((groups + 1,), jnp.int32)],
+        cost_estimate=pl.CostEstimate(flops=0, bytes_accessed=4_000_000, transcendentals=0),
+    )(table, near, order, weight_one.T, bias_one[None], weight_two.T, bias_two[None])
+
+
+def collect_kernel(owner_ref, part_ref, *refs):
+    sources, out_ref, sems = refs[:-2], refs[-2], refs[-1]
+    for k in range(out_ref.shape[0]):
+        for which, source in enumerate(sources):
+            @pl.when(part_ref[k] == which)
+            def _(k=k, source=source):
+                pltpu.make_async_copy(
+                    source.at[owner_ref[k]], out_ref.at[k], sems.at[k]
+                ).start()
+    for k in range(out_ref.shape[0]):
+        pltpu.make_async_copy(sources[0].at[0], out_ref.at[k], sems.at[k]).wait()
+
+
+def collect(owner, part, arrived, slot_count):
+    smem = pl.BlockSpec(memory_space=pltpu.SMEM)
+    anywhere = pl.BlockSpec(memory_space=pl.ANY)
+    return pl.pallas_call(
+        collect_kernel,
+        out_shape=jax.ShapeDtypeStruct((slot_count, 64, 512), BF),
+        in_specs=[smem, smem] + [anywhere] * len(arrived),
+        out_specs=anywhere,
+        scratch_shapes=[pltpu.SemaphoreType.DMA((slot_count,))],
+    )(owner, part, *arrived)
 
 
 def brick_kernel(
     n_ref, cols_ref, slots_ref, flags_ref,
     main_ref, prev_ref, next_ref, zmain_ref, zprev_ref, znext_ref, edge_ref,
-    spread_ref, inter_ref, w1_ref, b1_ref, w2_ref, b2_ref,
-    out_ref,
-    ext_ref, hid_ref, taps_ref, pool_ref,
-    *, columns,
+    spread_ref, inter_ref, w1_ref, b1_ref, w2_ref, b2_ref, *refs,
+    columns, begin,
 ):
-    step = pl.program_id(0)
+    out_ref, ext_ref, hid_ref, taps_ref, pool_ref = refs[-5:]
+    step = pl.program_id(0) + begin
 
     @pl.when(step < n_ref[0])
     def _():
@@ -168,14 +270,15 @@
 
 
 def compute_bricks(
-    count, cols, slots, flags, volume, zhalo, edge, w1, b1, w2, b2, out_slots, columns, steps
+    count, cols, slots, flags, volume, zhalo, edge, w1, b1, w2, b2, earlier,
+    groups, columns, begin, steps,
 ):
     spread = jnp.asarray(spread_matrix(), BF)
     inter = jnp.asarray(interleave_matrices(), BF)
 
     def at(shift):
         def index(i, n, c, s, f):
-            return (0, 0, jnp.clip(c[i] + shift, 0, columns - 1))
+            return (0, 0, jnp.clip(c[i + begin] + shift, 0, columns - 1))
         return index
 
     def whole(shape):
@@ -186,8 +289,9 @@
         grid=(steps,),
         in_specs=[pl.BlockSpec((SIDE, 64, 128), at(s)) for s in (0, -1, 1)]
         + [pl.BlockSpec((2, 64, 128), at(s)) for s in (0, -1, 1)]
-        + [whole(v.shape) for v in (edge, spread, inter, w1, b1, w2, b2)],
-        out_specs=pl.BlockSpec((1, 64, 512), lambda i, n, c, s, f: (s[i], 0, 0)),
+        + [whole(v.shape) for v in (edge, spread, inter, w1, b1, w2, b2)]
+        + [pl.BlockSpec(memory_space=pl.ANY)] * len(earlier),
+        out_specs=pl.BlockSpec((1, 64, 512), lambda i, n, c, s, f: (s[i + begin], 0, 0)),
         scratch_shapes=[
             pltpu.VMEM((34, 48, 256), F32),
             pltpu.VMEM((34, PITCH, 256), F32),
@@ -196,8 +300,8 @@
         ],
     )
     return pl.pallas_call(
-        functools.partial(brick_kernel, columns=columns),
-        out_shape=jax.ShapeDtypeStruct((out_slots, 64, 512), BF),
+        functools.partial(brick_kernel, columns=columns, begin=begin),
+        out_shape=jax.ShapeDtypeStruct((groups, 64, 512), BF),
         grid_spec=grid_spec,
         compiler_params=pltpu.CompilerParams(
             dimension_semantics=("arbitrary",), vmem_limit_bytes=48 * 1024 * 1024
@@ -206,7 +310,7 @@
             flops=steps * 1_600_000_000, bytes_accessed=steps * 1_600_000, transcendentals=0
         ),
     )(count, cols, slots, flags, volume, volume, volume, zhalo, zhalo, zhalo, edge,
-      spread, inter, w1, b1, w2, b2)
+      spread, inter, w1, b1, w2, b2, *earlier)
 
 
 MESH = pl.DeviceIdType.MESH
@@ -363,7 +467,7 @@
             dma((2,)), dma((groups,)), dma((groups,)), dma((8,)), dma((8,)), dma((8,)), dma((8,)),
         ],
         compiler_params=pltpu.CompilerParams(
-            collective_id=0, has_side_effects=True, vmem_limit_bytes=16 * 1024 * 1024
+            collective_id=0, has_side_effects=True, vmem_limit_bytes=56 * 1024 * 1024
         ),
         cost_estimate=pl.CostEstimate(flops=0, bytes_accessed=2_000_000, transcendentals=0),
     )(volume, occupancy)
@@ -373,64 +477,22 @@
     columns = occupancy.shape[1]
     slabs = lax.axis_size("gz")
     groups = lax.axis_size("xy")
-    capacity = (columns + groups - 1) // groups
-    slot_count = columns // 2
-    me = lax.axis_index("xy")
     zhalo, edge, table, near = exchange(volume, occupancy, slabs, groups, columns)
-    total = groups * columns
-    row = table[:, 0, :columns].reshape(total)
-    near = near[:, :, 0, :columns].reshape(3, 3 * columns)[:, columns - 1:2 * columns + 1]
-    own = occupancy[0]
-    order = device_order[0]
-    ids = jnp.arange(columns, dtype=jnp.int32)
-    labels = jnp.arange(groups, dtype=jnp.int32)
-    everyone = jnp.arange(total, dtype=jnp.int32)
-    local_rank = jnp.sum(jnp.where(ids[None, :] < ids[:, None], own[None, :], 0), axis=1)
-    start = jnp.sum(jnp.where(everyone < me * columns, row, 0))
-    label = (start + local_rank) % groups
-    target = jnp.sum(jnp.where(label[:, None] == labels[None, :], order[None, :], 0), axis=1)
-    count = jnp.sum(own)
-    flag_of = jnp.stack([near[a, b:b + columns] for a in range(3) for b in range(3)], axis=1)
-    early = min(columns, 2 * groups)
-
-    def part(begin, end):
-        amount = jnp.clip(count - begin, 0, end - begin)
-        wanted = begin + jnp.minimum(
-            jnp.arange(end - begin, dtype=jnp.int32), jnp.maximum(amount - 1, 0)
-        )
-        hit = (local_rank[None, :] == wanted[:, None]) & (own[None, :] > 0)
-        cols = jnp.sum(jnp.where(hit, ids[None, :], 0), axis=1)
-        part_capacity = (end - begin + groups - 1) // groups
-        slot = target * part_capacity + (local_rank - begin) // groups
-        slots = jnp.sum(jnp.where(hit, slot[None, :], 0), axis=1)
-        flags = jnp.sum(jnp.where(hit[:, :, None], flag_of[None], 0), axis=1).reshape(-1)
-        return amount.reshape(1), cols, slots, flags, part_capacity
-
-    w1 = banded(weight_one.reshape(64, 3, 3, 64).transpose(1, 2, 3, 0)).reshape(768, 256)
-    w2 = banded(weight_two.reshape(64, 3, 3, 3, 64).transpose(1, 2, 3, 4, 0)).reshape(2304, 256)
-    b1 = jnp.tile(bias_one, ACROSS)[None]
-    b2 = jnp.tile(bias_two, ACROSS)[None]
-
+    count, cols, slots, flags, owner, part, w1, b1, w2, b2 = plan(
+        table, near, device_order, weight_one, bias_one, weight_two, bias_two, groups, columns
+    )
     arrived = []
-    for begin, end in ((0, early), (early, columns)):
-        if begin < end:
-            amount, cols, slots, flags, part_capacity = part(begin, end)
-            made = compute_bricks(
-                amount, cols, slots, flags, volume, zhalo, edge, w1, b1, w2, b2,
-                groups * part_capacity, columns, end - begin,
-            )
-            sent = lax.all_to_all(made, "xy", split_axis=0, concat_axis=0, tiled=True)
-            arrived.append(sent.reshape(groups, part_capacity, 64, 512))
-    arrived = jnp.concatenate(arrived, axis=1).reshape(groups * capacity, 64, 512)
-
-    my_label = jnp.sum(jnp.where(order == me, labels, 0))
-    need = jnp.arange(slot_count, dtype=jnp.int32) * groups + my_label
-    counts = row.reshape(groups, columns).sum(axis=1)
-    starts = jnp.sum(jnp.where(labels[None, :] < labels[:, None], counts[None, :], 0), axis=1)
-    owner = jnp.sum(((starts + counts)[None, :] <= need[:, None]).astype(jnp.int32), axis=1)
-    owner_start = jnp.sum(jnp.where(labels[None, :] == owner[:, None], starts[None, :], 0), axis=1)
-    arrival = owner * capacity + (need - owner_start) // groups
-    return jnp.take(arrived, arrival, axis=0)
+    earlier = ()
+    for begin in range(0, columns, groups):
+        made = compute_bricks(
+            count, cols, slots, flags, volume, zhalo, edge, w1, b1, w2, b2, earlier,
+            groups, columns, begin, min(groups, columns - begin),
+        )
+        earlier = (made,)
+        arrived.append(
+            lax.all_to_all(made, "xy", split_axis=0, concat_axis=0, tiled=True)
+        )
+    return collect(owner, part, arrived, columns // 2)
 
 
 def solution(mesh):

time: 138 us -> 165 us (1.20)
  blocking collectives: 0 us -> 67 us
  waiting for transfers between devices: 24.3 us -> 1.14 us
  other arithmetic: 14.9 us -> 0 us
  starting transfers between devices: 10 us -> 4.8 us
  local copies, waits for them, and re-layouts: 9.62 us -> 12.4 us
    all_to_all x0 -> x2, blocking collectives: none -> 67 us  [per_device(): lax.all_to_all(made, 'xy', split_axis=0, concat_axis=0, tiled=True)]
    all_to_all x2 -> x1, waiting for transfers between devices: 24.3 us -> 1.14 us  [per_device(): lax.all_to_all(made, 'xy', split_axis=0, concat_axis=0, tiled=True)]
    unnamed x19 -> x44, local copies, waits for them, and re-layouts: 4.82 us -> 12.4 us
    concatenate x3 -> x0, other arithmetic: 5.9 us -> none  [the longest x2 4.72 us: banded(): return jnp.concatenate(rows, axis=-2)]
    all_to_all x2 -> x1, starting transfers between devices: 10 us -> 4.8 us  [per_device(): lax.all_to_all(made, 'xy', split_axis=0, concat_axis=0, tiled=True)]
    reduce_sum x12 -> x0, other arithmetic: 4.68 us -> none  [the longest x1 1.26 us: per_device(): count = jnp.sum(own)]
    slice x5 -> x0, local copies, waits for them, and re-layouts: 3.06 us -> none  [the longest x4 3.04 us: banded(): blocks.append(taps[..., tap, :, :] if 0 <= tap < 3 else zero)]
    select_n x3 -> x0, other arithmetic: 2.28 us -> none  [the longest x2 1.62 us: per_device(): return jnp.take(arrived, arrival, axis=0)]
  transfers between devices with their start and end apart: 2 -> 1, of which waited for: 1 -> 1; matrix products, arithmetic and copies ran while one was open for 3% -> 0% of each run, Pallas kernels for 39% -> 7%
where the time goes in v4:
time: 165 us
  Pallas kernels  79.4 us (48%)
  blocking collectives  67 us (41%)
  local copies, waits for them, and re-layouts  12.4 us (8%)
  starting transfers between devices  4.8 us (3%)
    all_to_all x2, blocking collectives, per_device(): lax.all_to_all(made, 'xy', split_axis=0, concat_axis=0, tiled=True)  67 us
    pallas_call x3, Pallas kernels, compute_bricks(): pl.pallas_call(functools.partial(brick_kernel, columns=columns, begin=beg...  40.7 us
    pallas_call x1, Pallas kernels, collect(): pl.pallas_call(collect_kernel, out_shape=jax.ShapeDtypeStruct((slot_count...  21.7 us
    unnamed x44, local copies, waits for them, and re-layouts  12.4 us
    pallas_call x1, Pallas kernels, exchange(): pl.pallas_call(functools.partial(exchange_kernel, slabs=slabs, groups=gro...  11.3 us
    pallas_call x1, Pallas kernels, plan(): pl.pallas_call(functools.partial(plan_kernel, groups=groups, columns=colu...  5.69 us
    all_to_all x1, starting transfers between devices, per_device(): lax.all_to_all(made, 'xy', split_axis=0, concat_axis=0, tiled=True)  4.8 us
  transfers between devices with their start and end apart: 1, of which 1 were waited for; matrix products, arithmetic and copies ran while one was open for 0% of the time, Pallas kernels for 7%

profile of v4, /device:TPU:0, one launch (start us, length us, event | category | flops | bytes accessed | tf_op | source)
XLA Modules:
  0.0 164.8 jit_solution(13132510457374715326)
XLA Ops:
  0.0 0.0 copy-start.6
  0.0 0.0 copy-start.10
  0.0 1.7 %copy.14 = bf16[64,576]{0,1:T(8,128)(2,1)} copy(bf16[64,576]{1,0:T(8,128)(2,1)} %param.16) | data formatting | bytes 147456 | tf_op args[3]
  1.7 1.9 %copy.15 = bf16[64,1728]{0,1:T(8,128)(2,1)} copy(bf16[64,1728]{1,0:T(8,128)(2,1)} %param.18) | data formatting | bytes 442368 | tf_op args[5]
  3.6 11.3 %shard_map.127 = (bf16[2,64,2560]{2,1,0:T(8,128)(2,1)}, bf16[34,64,128]{2,1,0:T(8,128)(2,1)}, s32[8,8,128]{2,1,0:T(8,128)}, s32[3,3,8,128]{3,2,1,0:T(8,128)}) custom-call(bf16[32,64,2560]{2,1,0:T(8,128)(2,1)} %next_ref.5, s32[1,20]{1,0:T(1,128)} %occ_ref.1), custom_call_target="tpu_custom_call" | custom-call | bytes 2000000 | tf_op jit(solution)/shard_map/pallas_call | solution.py:450
  14.9 5.7 %shard_map.128 = (s32[1]{0:T(128)}, s32[21]{0:T(128)}, s32[21]{0:T(128)}, s32[189]{0:T(256)}, s32[10]{0:T(128)}, /*index=5*/s32[10]{0:T(128)}, bf16[768,256]{1,0...) custom-call(s32[8,8,128]{2,1,0:T(8,128)} %get-tuple-element.19.table_ref, ...), custom_call_target="tpu_custom_call" | custom-call | bytes 4000000 | tf_op jit(solution)/shard_map/pallas_call | solution.py:111
  20.6 0.0 copy-done.6
  20.6 0.0 copy-done.10
  20.6 0.0 copy-start
  20.7 1.1 copy-done
  21.7 0.0 copy-start.2
  21.7 1.3 copy-done.2
  23.0 0.0 copy-start.4
  23.0 1.1 copy-done.4
  24.1 0.0 copy-start.8
  24.1 1.0 copy-done.8
  25.1 0.0 copy-start.11
  25.1 0.7 copy-done.11
  25.7 0.0 copy-start.13
  25.7 0.7 copy-done.13
  26.4 0.0 copy-start.15
  26.4 0.7 copy-done.15
  27.1 0.0 copy-start.17
  27.1 0.6 copy-done.17
  27.7 0.0 copy-start.19
  27.7 0.7 copy-done.19
  28.3 0.0 copy-start.1
  28.4 0.0 copy-start.3
  28.4 0.0 copy-start.5
  28.4 0.0 copy-start.12
  28.4 0.0 copy-start.14
  28.4 0.0 copy-start.16
  28.4 0.0 copy-start.18
  28.4 0.0 copy-start.20
  28.4 28.6 %shard_map.129.refs_0_ = bf16[8,64,512]{2,1,0:T(8,128)(2,1)} custom-call(s32[1]{0:T(128)} %get-tuple-element.23.n_ref, s32[21]{0:T(128)S(1)} %copy-done.17, s32[21]{0:T(128)S(1)} %copy-done.19, s32[189]{0:T(256)S(1)} %copy-done.11, bf16[32,64,2560]{2,1,0:T(8,128)(2,1)} %next_ref.5, bf16[32,64,2560]{2,1,0:T(8,128)(2,1)} %next_ref.5, ...), custom_call_target="tpu_custom_call" | custom-call | flops 12800000000 | bytes 12800000 | tf_op jit(solution)/shard_map/pallas_call | solution.py:302
  57.0 4.8 %all-to-all-start = ((bf16[8,64,512]{2,1,0:T(8,128)(2,1)}), bf16[8,64,512]{2,1,0:T(8,128)(2,1)}, u32[]{:S(2)}, u32[]{:S(2)}) async-start(bf16[8,64,512]{2,1,0:T(8,128)(2,1)} %shard_map.129.refs_0_), calls=%async_computation | async-start | bytes 1048576 | tf_op jit(solution)/shard_map/all_to_all | solution.py:493
  61.8 0.0 copy-done.1
  61.8 0.0 copy-done.3
  61.8 0.0 copy-done.5
  61.9 0.0 copy-done.12
  61.9 0.0 copy-done.14
  61.9 0.0 copy-done.16
  61.9 0.0 copy-done.18
  61.9 0.0 copy-done.20
  61.9 0.0 copy-start.9
  61.9 1.0 copy-done.9
  62.9 0.0 copy-start.7
  62.9 9.4 %shard_map.130.refs_0_ = bf16[8,64,512]{2,1,0:T(8,128)(2,1)S(1)} custom-call(s32[1]{0:T(128)} %get-tuple-element.23.n_ref, s32[21]{0:T(128)S(1)} %copy-done.18, s32[21]{0:T(128)S(1)} %copy-done.20, s32[189]{0:T(256)S(1)} %copy-done.12, bf16[32,64,2560]{2,1,0:T(8,128)(2,1)} %next_ref.5, bf16[32,64,2560]{2,1,0:T(8,128)(2,1)} %next_ref.5, ...), custom_call_target="tpu_custom_call" | custom-call | flops 12800000000 | bytes 12800000 | tf_op jit(solution)/shard_map/pallas_call | solution.py:302
  72.3 0.0 copy-done.7
  72.3 2.6 %shard_map.131 = bf16[8,64,512]{2,1,0:T(8,128)(2,1)S(1)} custom-call(s32[1]{0:T(128)} %get-tuple-element.23.n_ref, s32[21]{0:T(128)S(1)} %copy-done.18, s32[21]{0:T(128)S(1)} %copy-done.20, s32[189]{0:T(256)S(1)} %copy-done.12, bf16[32,64,2560]{2,1,0:T(8,128)(2,1)} %next_ref.5, bf16[32,64,2560]{2,1,0:T(8,128)(2,1)} %next_ref.5, ...), custom_call_target="tpu_custom_call" | custom-call | flops 6400000000 | bytes 6400000 | tf_op jit(solution)/shard_map/pallas_call | solution.py:302
  75.0 1.1 all-to-all-done.refs_0_
  76.1 47.7 %all_to_all.15.refs_2_ = bf16[8,64,512]{2,1,0:T(8,128)(2,1)} all-to-all(bf16[8,64,512]{2,1,0:T(8,128)(2,1)S(1)} %shard_map.131), channel_id=1, replica_groups=mesh['gz'=4,'xy'=8] {'xy'}, dimensions={0} | all-to-all | bytes 1048576 | tf_op jit(solution)/shard_map/all_to_all | solution.py:493
  123.8 19.3 %all_to_all.16.refs_1_ = bf16[8,64,512]{2,1,0:T(8,128)(2,1)} all-to-all(bf16[8,64,512]{2,1,0:T(8,128)(2,1)S(1)} %shard_map.130.refs_0_), channel_id=1, replica_groups=mesh['gz'=4,'xy'=8] {'xy'}, dimensions={0} | all-to-all | bytes 1048576 | tf_op jit(solution)/shard_map/all_to_all | solution.py:493
  143.1 21.7 %shard_map.132 = bf16[10,64,512]{2,1,0:T(8,128)(2,1)} custom-call(s32[10]{0:T(128)} %get-tuple-element.21.owner_ref, s32[10]{0:T(128)} %get-tuple-element.22.part_ref, bf16[8,64,512]{2,1,0:T(8,128)(2,1)} %all-to-all-done.refs_0_, bf16[8,64,512]{2,1,0:T(8,128)(2,1)} %all_to_all.16.refs_1_, bf16[8,64,512]{2,1,0:T(8,128)(2,1)} %all_to_all.15.refs_2_), custom_call_target="tpu_custom_call" | custom-call | tf_op jit(solution)/shard_map/pallas_call | solution.py:142
Async XLA Ops:
  0.0 20.6 %copy-start.6 = (bf16[2,256,512]{2,1,0:T(8,128)(2,1)S(1)}, bf16[2,256,512]{2,1,0:T(8,128)(2,1)}, u32[]{:S(2)}) copy-start(bf16[2,256,512]{2,1,0:T(8,128)(2,1)} %constant.5.clone.inter_ref) | copy-start | bytes 1572868
  0.0 20.6 %copy-start.10 = (bf16[160,256]{1,0:T(8,128)(2,1)S(1)}, bf16[160,256]{1,0:T(8,128)(2,1)}, u32[]{:S(2)}) copy-start(bf16[160,256]{1,0:T(8,128)(2,1)} %constant.4.clone.spread_ref) | copy-start | bytes 245764
  20.6 1.1 copy-start
  21.7 1.3 copy-start.2
  23.0 1.1 copy-start.4
  24.1 1.0 copy-start.8
  25.1 0.7 copy-start.11
  25.7 0.7 copy-start.13
  26.4 0.7 copy-start.15
  27.1 0.6 copy-start.17
  27.7 0.7 copy-start.19
  28.3 33.5 %copy-start.1 = (bf16[2,64,2560]{2,1,0:T(8,128)(2,1)S(1)}, bf16[2,64,2560]{2,1,0:T(8,128)(2,1)}, u32[]{:S(2)}) copy-start(bf16[2,64,2560]{2,1,0:T(8,128)(2,1)} %get-tuple-element.27.zmain_ref.zprev_ref.znext_ref) | copy-start | bytes 1966084
  28.4 33.5 %copy-start.3 = (bf16[2304,256]{1,0:T(8,128)(2,1)S(1)}, bf16[2304,256]{1,0:T(8,128)(2,1)}, u32[]{:S(2)}) copy-start(bf16[2304,256]{1,0:T(8,128)(2,1)} %get-tuple-element.31.w2_ref) | copy-start | bytes 3538948
  28.4 33.5 %copy-start.5 = (bf16[34,64,128]{2,1,0:T(8,128)(2,1)S(1)}, bf16[34,64,128]{2,1,0:T(8,128)(2,1)}, u32[]{:S(2)}) copy-start(bf16[34,64,128]{2,1,0:T(8,128)(2,1)} %get-tuple-element.28.edge_ref) | copy-start | bytes 1671172
  28.4 33.5 %copy-start.12 = (s32[189]{0:T(256)S(1)}, s32[189]{0:T(256)}, u32[]{:S(2)}) copy-start(s32[189]{0:T(256)} %get-tuple-element.26.flags_ref) | copy-start | bytes 2272
  28.4 33.5 %copy-start.14 = (f32[1,256]{1,0:T(1,128)S(1)}, f32[1,256]{1,0:T(1,128)}, u32[]{:S(2)}) copy-start(f32[1,256]{1,0:T(1,128)} %get-tuple-element.30.b1_ref) | copy-start | bytes 3076
  28.4 33.5 %copy-start.16 = (f32[1,256]{1,0:T(1,128)S(1)}, f32[1,256]{1,0:T(1,128)}, u32[]{:S(2)}) copy-start(f32[1,256]{1,0:T(1,128)} %get-tuple-element.32.b2_ref) | copy-start | bytes 3076
  28.4 33.5 %copy-start.18 = (s32[21]{0:T(128)S(1)}, s32[21]{0:T(128)}, u32[]{:S(2)}) copy-start(s32[21]{0:T(128)} %get-tuple-element.24.cols_ref) | copy-start | bytes 256
  28.4 33.5 %copy-start.20 = (s32[21]{0:T(128)S(1)}, s32[21]{0:T(128)}, u32[]{:S(2)}) copy-start(s32[21]{0:T(128)} %get-tuple-element.25.slots_ref) | copy-start | bytes 256
  57.0 19.1 %all-to-all-start = ((bf16[8,64,512]{2,1,0:T(8,128)(2,1)}), bf16[8,64,512]{2,1,0:T(8,128)(2,1)}, u32[]{:S(2)}, u32[]{:S(2)}) async-start(bf16[8,64,512]{2,1,0:T(8,128)(2,1)} %shard_map.129.refs_0_), calls=%async_computation | async-start | bytes 1048576 | tf_op jit(solution)/shard_map/all_to_all | solution.py:493
  61.9 1.0 copy-start.9
  62.9 9.4 %copy-start.7 = (bf16[2,256,512]{2,1,0:T(8,128)(2,1)S(1)}, bf16[2,256,512]{2,1,0:T(8,128)(2,1)}, u32[]{:S(2)}) copy-start(bf16[2,256,512]{2,1,0:T(8,128)(2,1)} %constant.5.clone.inter_ref) | copy-start | bytes 1572868

commit v5 on v3

--- a/solution.py
+++ b/solution.py
@@ -48,11 +48,10 @@
 def brick_kernel(
     n_ref, cols_ref, slots_ref, flags_ref,
     main_ref, prev_ref, next_ref, zmain_ref, zprev_ref, znext_ref, edge_ref,
-    spread_ref, inter_ref, w1_ref, b1_ref, w2_ref, b2_ref,
-    out_ref,
-    ext_ref, hid_ref, taps_ref, pool_ref,
-    *, columns,
+    spread_ref, inter_ref, w1_ref, b1_ref, w2_ref, b2_ref, *refs,
+    columns,
 ):
+    out_ref, ext_ref, hid_ref, taps_ref, pool_ref = refs[-5:]
     step = pl.program_id(0)
 
     @pl.when(step < n_ref[0])
@@ -168,7 +167,7 @@
 
 
 def compute_bricks(
-    count, cols, slots, flags, volume, zhalo, edge, w1, b1, w2, b2, out_slots, columns, steps
+    count, cols, slots, flags, volume, zhalo, edge, w1, b1, w2, b2, earlier, out_slots, columns, steps
 ):
     spread = jnp.asarray(spread_matrix(), BF)
     inter = jnp.asarray(interleave_matrices(), BF)
@@ -186,7 +185,8 @@
         grid=(steps,),
         in_specs=[pl.BlockSpec((SIDE, 64, 128), at(s)) for s in (0, -1, 1)]
         + [pl.BlockSpec((2, 64, 128), at(s)) for s in (0, -1, 1)]
-        + [whole(v.shape) for v in (edge, spread, inter, w1, b1, w2, b2)],
+        + [whole(v.shape) for v in (edge, spread, inter, w1, b1, w2, b2)]
+        + [pl.BlockSpec(memory_space=pl.ANY)] * len(earlier),
         out_specs=pl.BlockSpec((1, 64, 512), lambda i, n, c, s, f: (s[i], 0, 0)),
         scratch_shapes=[
             pltpu.VMEM((34, 48, 256), F32),
@@ -206,7 +206,7 @@
             flops=steps * 1_600_000_000, bytes_accessed=steps * 1_600_000, transcendentals=0
         ),
     )(count, cols, slots, flags, volume, volume, volume, zhalo, zhalo, zhalo, edge,
-      spread, inter, w1, b1, w2, b2)
+      spread, inter, w1, b1, w2, b2, *earlier)
 
 
 MESH = pl.DeviceIdType.MESH
@@ -373,7 +373,6 @@
     columns = occupancy.shape[1]
     slabs = lax.axis_size("gz")
     groups = lax.axis_size("xy")
-    capacity = (columns + groups - 1) // groups
     slot_count = columns // 2
     me = lax.axis_index("xy")
     zhalo, edge, table, near = exchange(volume, occupancy, slabs, groups, columns)
@@ -391,7 +390,7 @@
     target = jnp.sum(jnp.where(label[:, None] == labels[None, :], order[None, :], 0), axis=1)
     count = jnp.sum(own)
     flag_of = jnp.stack([near[a, b:b + columns] for a in range(3) for b in range(3)], axis=1)
-    early = min(columns, 2 * groups)
+    early = columns - groups
 
     def part(begin, end):
         amount = jnp.clip(count - begin, 0, end - begin)
@@ -412,16 +411,18 @@
     b2 = jnp.tile(bias_two, ACROSS)[None]
 
     arrived = []
+    earlier = ()
     for begin, end in ((0, early), (early, columns)):
         if begin < end:
             amount, cols, slots, flags, part_capacity = part(begin, end)
             made = compute_bricks(
                 amount, cols, slots, flags, volume, zhalo, edge, w1, b1, w2, b2,
-                groups * part_capacity, columns, end - begin,
+                earlier, groups * part_capacity, columns, end - begin,
             )
+            earlier = (made,)
             sent = lax.all_to_all(made, "xy", split_axis=0, concat_axis=0, tiled=True)
             arrived.append(sent.reshape(groups, part_capacity, 64, 512))
-    arrived = jnp.concatenate(arrived, axis=1).reshape(groups * capacity, 64, 512)
+    arrived = jnp.concatenate(arrived, axis=1).reshape(-1, 64, 512)
 
     my_label = jnp.sum(jnp.where(order == me, labels, 0))
     need = jnp.arange(slot_count, dtype=jnp.int32) * groups + my_label
@@ -429,8 +430,10 @@
     starts = jnp.sum(jnp.where(labels[None, :] < labels[:, None], counts[None, :], 0), axis=1)
     owner = jnp.sum(((starts + counts)[None, :] <= need[:, None]).astype(jnp.int32), axis=1)
     owner_start = jnp.sum(jnp.where(labels[None, :] == owner[:, None], starts[None, :], 0), axis=1)
-    arrival = owner * capacity + (need - owner_start) // groups
-    return jnp.take(arrived, arrival, axis=0)
+    rank = need - owner_start
+    early_rows = (early + groups - 1) // groups
+    place = jnp.where(rank < early, rank // groups, early_rows + (rank - early) // groups)
+    return jnp.take(arrived, owner * (early_rows + 1) + place, axis=0, mode="clip")
 
 
 def solution(mesh):

time: 138 us -> 146 us (1.058)
  blocking collectives: 0 us -> 22.3 us
  starting transfers between devices: 10 us -> 4.33 us
  other arithmetic: 14.9 us -> 9.66 us
  Pallas kernels: 78.8 us -> 76.3 us
    all_to_all x0 -> x1, blocking collectives: none -> 22.3 us  [per_device(): sent = lax.all_to_all(made, 'xy', split_axis=0, concat_axis=0, tiled=True)]
    all_to_all x2 -> x1, starting transfers between devices: 10 us -> 4.33 us  [per_device(): sent = lax.all_to_all(made, 'xy', split_axis=0, concat_axis=0, tiled=True)]
    pallas_call x2, Pallas kernels: 68.8 us -> 66.3 us  [compute_bricks(): pl.pallas_call(functools.partial(brick_kernel, columns=columns), out_shap...]
    slice x4, local copies, waits for them, and re-layouts: 3.04 us -> 1.14 us  [banded(): blocks.append(taps[..., tap, :, :] if 0 <= tap < 3 else zero)]
    select_n x2 -> x0, other arithmetic: 1.62 us -> none  [per_device(): return jnp.take(arrived, arrival, axis=0)]
    all_to_all x2 -> x1, waiting for transfers between devices: 24.3 us -> 23.8 us  [per_device(): sent = lax.all_to_all(made, 'xy', split_axis=0, concat_axis=0, tiled=True)]
    unnamed x19 -> x21, local copies, waits for them, and re-layouts: 4.82 us -> 4.82 us
  transfers between devices with their start and end apart: 2 -> 1, of which waited for: 1 -> 1; matrix products, arithmetic and copies ran while one was open for 3% -> 2% of each run, Pallas kernels for 39% -> 0%
where the time goes in v5:
time: 146 us; the launch traced here: 147 us
  Pallas kernels  76.3 us (52%)
  waiting for transfers between devices  23.8 us (16%)
  blocking collectives  22.3 us (15%)
  other arithmetic  9.66 us (7%)
  local copies, waits for them, and re-layouts  8.59 us (6%)
  starting transfers between devices  4.33 us (3%)
  between operations  1.59 us (1%)
    pallas_call x2, Pallas kernels, compute_bricks(): pl.pallas_call(functools.partial(brick_kernel, columns=columns), out_shap...  66.3 us
    all_to_all x1, waiting for transfers between devices, per_device(): sent = lax.all_to_all(made, 'xy', split_axis=0, concat_axis=0, tiled=True)  23.8 us
    all_to_all x1, blocking collectives, per_device(): sent = lax.all_to_all(made, 'xy', split_axis=0, concat_axis=0, tiled=True)  22.3 us
    pallas_call x1, Pallas kernels, exchange(): pl.pallas_call(functools.partial(exchange_kernel, slabs=slabs, groups=gro...  9.97 us
    unnamed x21, local copies, waits for them, and re-layouts  4.82 us
    all_to_all x1, starting transfers between devices, per_device(): sent = lax.all_to_all(made, 'xy', split_axis=0, concat_axis=0, tiled=True)  4.33 us
    concatenate x2, other arithmetic, banded(): return jnp.concatenate(rows, axis=-2)  3.47 us
  transfers between devices with their start and end apart: 1, of which 1 were waited for; matrix products, arithmetic and copies ran while one was open for 2% of the time, Pallas kernels for 0%

profile of v5, /device:TPU:0, one launch (start us, length us, event | category | flops | bytes accessed | tf_op | source)
XLA Modules:
  0.0 146.6 jit_solution(10497202387957180198)
XLA Ops:
  0.0 0.7 compare_bitcast_fusion
  0.7 0.0 copy-start
  0.7 4.0 %copy-done = bf16[32,64,2560]{2,1,0:T(8,128)(2,1)S(1)} copy-done((bf16[32,64,2560]{2,1,0:T(8,128)(2,1)S(1)}, bf16[32,64,2560]{2,1,0:T(8,128)(2,1)}, u32[]{:S(2)}) %copy-start) | copy-done | bytes 10485784
  4.6 0.0 copy-start.1
  4.6 0.7 copy-done.1
  5.3 0.0 copy-start.2
  5.3 0.0 copy-start.9
  5.3 0.0 copy-start.5
  5.3 10.0 %shard_map.109 = (bf16[2,64,2560]{2,1,0:T(8,128)(2,1)S(1)}, bf16[34,64,128]{2,1,0:T(8,128)(2,1)S(1)}, s32[8,8,128]{2,1,0:T(8,128)S(1)}, s32[3,3,8,128]{3,2,1,0:T(8,128)S(1)}) custom-call(bf16[32,64,2560]{2,1,0:T(8,128)(2,1)S(1)} %copy-done, s32[1,20]{1,0:T(1,128)S(1)} %copy-done.1), custom_call_target="tpu_custom_call" | custom-call | bytes 2000000 | tf_op jit(solution)/shard_map/pallas_call | solution.py:346
  15.3 0.0 copy-start.6
  15.3 0.0 copy-start.7
  15.3 0.0 copy-start.8
  15.3 0.1 reshape_squeeze.4
  15.4 0.1 slice_bitcast_fusion.3
  15.5 0.0 copy-done.2
  15.5 0.1 select_reduce_fusion.2
  15.6 0.8 slice_reduce_fusion.1
  16.4 0.7 and_select_fusion.4
  17.1 0.0 copy-done.9
  17.1 0.1 select_reduce_fusion.9
  17.2 0.6 reduce_sum.137
  18.5 0.2 select_reduce_fusion.3
  18.7 0.2 select_reduce_fusion
  19.0 0.1 copy.62
  19.1 0.1 reshape.336.flags_ref
  19.1 0.0 copy-done.5
  19.2 0.3 reshape.339
  19.5 0.6 fusion.6
  20.1 0.0 copy-start.3
  20.2 0.0 copy-start.4
  20.2 0.2 copy.66
  20.3 0.2 copy.67
  20.5 0.2 copy.68
  20.7 0.0 copy-done.6
  20.7 0.1 copy.63
  20.9 0.0 copy-done.7
  20.9 0.1 broadcast_in_dim_tile.6.b1_ref
  21.0 0.0 copy-done.8
  21.0 0.1 broadcast_in_dim_tile.7.b2_ref
  21.7 0.2 select_reduce_fusion.7
  21.9 0.2 select_reduce_fusion.1
  22.2 0.1 copy.69
  22.2 0.1 reshape.343.flags_ref
  22.4 3.3 %maximum_maximum_fusion = bf16[3,3,256,256]{3,2,1,0:T(8,128)(2,1)S(1)} fusion(bf16[3,3,64,64]{3,2,1,0:T(8,128)(2,1)S(1)} %bitcast.69, bf16[3,3,64,64]{3,2,1,0:T(8,128)(2,1)S(1)} %bitcast.71, bf16[3,3,64,128]{3,2,1,0:T(8,128)(2,1)S(1)} %broadcast.392, bf16[3,3,64,64]{3,2,1,0:T(8,128)(2,1)S(1)} %bitcast.70, bf16[3,3,64,64]{3,2,1,0:T(8,128)(2,1)S(1)} %broadcast_in_dim.182), kind=kLoop, calls=%fused_computation.2 | loop fusion | flops 16515072 | bytes 1622016 | tf_op jit(solution)/shard_map/concatenate | solution.py:45
  25.7 0.2 maximum_maximum_fusion.1
  25.9 0.0 copy-done.3
  25.9 0.0 copy-done.4
  25.9 41.6 %shard_map.110.refs_0_ = bf16[16,64,512]{2,1,0:T(8,128)(2,1)} custom-call(s32[1]{0:T(128)} %bitcast.n_ref, s32[12]{0:T(128)S(1)} %get-tuple-element.16.cols_ref, s32[12]{0:T(128)S(1)} %get-tuple-element.15.slots_ref, s32[108]{0:T(128)S(1)} %reshape.336.flags_ref, bf16[32,64,2560]{2,1,0:T(8,128)(2,1)} %next_ref.3, bf16[32,64,2560]{2,1,0:T(8,128)(2,1)} %next_ref.3, ...), custom_call_target="tpu_custom_call" | custom-call | flops 19200000000 | bytes 19200000 | tf_op jit(solution)/shard_map/pallas_call | solution.py:198
  67.6 24.7 %shard_map.111 = bf16[8,64,512]{2,1,0:T(8,128)(2,1)S(1)} custom-call(s32[1]{0:T(128)} %bitcast.26.n_ref, s32[8]{0:T(128)S(1)} %get-tuple-element.18.cols_ref, s32[8]{0:T(128)S(1)} %get-tuple-element.17.slots_ref, s32[72]{0:T(128)S(1)} %reshape.343.flags_ref, bf16[32,64,2560]{2,1,0:T(8,128)(2,1)} %next_ref.3, bf16[32,64,2560]{2,1,0:T(8,128)(2,1)} %next_ref.3, ...), custom_call_target="tpu_custom_call" | custom-call | flops 12800000000 | bytes 12800000 | tf_op jit(solution)/shard_map/pallas_call | solution.py:198
  92.3 22.3 %all_to_all.10 = bf16[8,64,512]{2,1,0:T(8,128)(2,1)S(1)} all-to-all(bf16[8,64,512]{2,1,0:T(8,128)(2,1)S(1)} %shard_map.111), channel_id=1, replica_groups=mesh['gz'=4,'xy'=8] {'xy'}, dimensions={0} | all-to-all | bytes 1048576 | tf_op jit(solution)/shard_map/all_to_all | solution.py:423
  114.6 4.3 %all-to-all-start = ((bf16[16,64,512]{2,1,0:T(8,128)(2,1)}), bf16[16,64,512]{2,1,0:T(8,128)(2,1)S(1)}, u32[]{:S(2)}, u32[]{:S(2)}) async-start(bf16[16,64,512]{2,1,0:T(8,128)(2,1)} %shard_map.110.refs_0_), calls=%async_computation | async-start | bytes 2097152 | tf_op jit(solution)/shard_map/all_to_all | solution.py:423
  118.9 0.1 select_reduce_fusion.6
  119.0 0.6 fusion.1
  119.6 0.6 multiply_add_fusion
  120.3 0.1 convert_reduce_fusion
  120.4 0.1 select_reduce_fusion.5
  120.5 0.7 fusion.3
  121.2 23.8 %all-to-all-done = bf16[16,64,512]{2,1,0:T(8,128)(2,1)S(1)} async-done(((bf16[16,64,512]{2,1,0:T(8,128)(2,1)}), bf16[16,64,512]{2,1,0:T(8,128)(2,1)S(1)}, u32[]{:S(2)}, u32[]{:S(2)}) %all-to-all-start) | async-done | bytes 1048608 | tf_op jit(solution)/shard_map/all_to_all | solution.py:423
  145.0 0.1 pad_maximum_fusion
  145.1 1.5 gather_fusion
  (14 shorter events, 0.2 us)
Async XLA Ops:
  0.7 4.0 %copy-start = (bf16[32,64,2560]{2,1,0:T(8,128)(2,1)S(1)}, bf16[32,64,2560]{2,1,0:T(8,128)(2,1)}, u32[]{:S(2)}) copy-start(bf16[32,64,2560]{2,1,0:T(8,128)(2,1)} %next_ref.3) | copy-start | bytes 31457284
  4.6 0.7 copy-start.1
  5.3 10.2 %copy-start.2 = (s32[1,20]{1,0:T(1,128)S(1)}, s32[1,20]{1,0:T(1,128)}, u32[]{:S(2)}) copy-start(s32[1,20]{1,0:T(1,128)} %occ_ref.1) | copy-start | bytes 244
  5.3 11.8 %copy-start.9 = (s32[1,8]{1,0:T(1,128)S(1)}, s32[1,8]{1,0:T(1,128)}, u32[]{:S(2)}) copy-start(s32[1,8]{1,0:T(1,128)} %param.13) | copy-start | bytes 100
  5.3 13.8 %copy-start.5 = (bf16[64,1728]{1,0:T(8,128)(2,1)S(1)}, bf16[64,1728]{1,0:T(8,128)(2,1)}, u32[]{:S(2)}) copy-start(bf16[64,1728]{1,0:T(8,128)(2,1)} %param.16) | copy-start | bytes 663556
  15.3 5.4 %copy-start.6 = (bf16[64,576]{1,0:T(8,128)(2,1)S(1)}, bf16[64,576]{1,0:T(8,128)(2,1)}, u32[]{:S(2)}) copy-start(bf16[64,576]{1,0:T(8,128)(2,1)} %param.14) | copy-start | bytes 221188
  15.3 5.6 %copy-start.7 = (f32[64]{0:T(128)S(1)}, f32[64]{0:T(128)}, u32[]{:S(2)}) copy-start(f32[64]{0:T(128)} %param.15) | copy-start | bytes 772
  15.3 5.7 %copy-start.8 = (f32[64]{0:T(128)S(1)}, f32[64]{0:T(128)}, u32[]{:S(2)}) copy-start(f32[64]{0:T(128)} %param.17) | copy-start | bytes 772
  20.1 5.8 %copy-start.3 = (bf16[2,256,512]{2,1,0:T(8,128)(2,1)S(1)}, bf16[2,256,512]{2,1,0:T(8,128)(2,1)}, u32[]{:S(2)}) copy-start(bf16[2,256,512]{2,1,0:T(8,128)(2,1)} %constant.89.clone.inter_ref) | copy-start | bytes 1572868
  20.2 5.8 %copy-start.4 = (bf16[160,256]{1,0:T(8,128)(2,1)S(1)}, bf16[160,256]{1,0:T(8,128)(2,1)}, u32[]{:S(2)}) copy-start(bf16[160,256]{1,0:T(8,128)(2,1)} %constant.88.clone.spread_ref) | copy-start | bytes 245764
  114.6 30.4 %all-to-all-start = ((bf16[16,64,512]{2,1,0:T(8,128)(2,1)}), bf16[16,64,512]{2,1,0:T(8,128)(2,1)S(1)}, u32[]{:S(2)}, u32[]{:S(2)}) async-start(bf16[16,64,512]{2,1,0:T(8,128)(2,1)} %shard_map.110.refs_0_), calls=%async_computation | async-start | bytes 2097152 | tf_op jit(solution)/shard_map/all_to_all | solution.py:423

commit v6 on v3

--- a/solution.py
+++ b/solution.py
@@ -430,7 +430,7 @@
     owner = jnp.sum(((starts + counts)[None, :] <= need[:, None]).astype(jnp.int32), axis=1)
     owner_start = jnp.sum(jnp.where(labels[None, :] == owner[:, None], starts[None, :], 0), axis=1)
     arrival = owner * capacity + (need - owner_start) // groups
-    return jnp.take(arrived, arrival, axis=0)
+    return jnp.take(arrived, arrival, axis=0, mode="clip")
 
 
 def solution(mesh):

time: 138 us -> 138 us (level); the launches traced: 139 us -> 137 us
  other arithmetic: 14.9 us -> 13.2 us
    select_n x2 -> x0, other arithmetic: 1.62 us -> none  [per_device(): return jnp.take(arrived, arrival, axis=0)]
  transfers between devices with their start and end apart: 2 -> 2, of which waited for: 1 -> 1; matrix products, arithmetic and copies ran while one was open for 3% -> 2% of each run, Pallas kernels for 39% -> 39%
where the time goes in v6:
time: 138 us; the launch traced here: 137 us
  Pallas kernels  78.8 us (57%)
  waiting for transfers between devices  24.3 us (18%)
  other arithmetic  13.2 us (10%)
  local copies, waits for them, and re-layouts  10.5 us (8%)
  starting transfers between devices  9.15 us (7%)
    pallas_call x2, Pallas kernels, compute_bricks(): pl.pallas_call(functools.partial(brick_kernel, columns=columns), out_shap...  68.8 us
    all_to_all x2, waiting for transfers between devices, per_device(): sent = lax.all_to_all(made, 'xy', split_axis=0, concat_axis=0, tiled=True)  24.3 us
    pallas_call x1, Pallas kernels, exchange(): pl.pallas_call(functools.partial(exchange_kernel, slabs=slabs, groups=gro...  9.98 us
    all_to_all x2, starting transfers between devices, per_device(): sent = lax.all_to_all(made, 'xy', split_axis=0, concat_axis=0, tiled=True)  9.15 us
    unnamed x19, local copies, waits for them, and re-layouts  4.82 us
    concatenate x2, other arithmetic, banded(): return jnp.concatenate(rows, axis=-2)  4.72 us
    slice x4, local copies, waits for them, and re-layouts, banded(): blocks.append(taps[..., tap, :, :] if 0 <= tap < 3 else zero)  3.04 us
  transfers between devices with their start and end apart: 2, of which 1 were waited for; matrix products, arithmetic and copies ran while one was open for 2% of the time, Pallas kernels for 39%

profile of v6, /device:TPU:0, one launch (start us, length us, event | category | flops | bytes accessed | tf_op | source)
XLA Modules:
  0.0 137.3 jit_solution(5286008215487144102)
XLA Ops:
  0.0 0.7 compare_bitcast_fusion
  0.7 1.3 reduce_sum.137
  2.5 0.8 select_reduce_fusion.2
  3.2 0.0 copy-start
  3.3 4.0 %copy-done = bf16[32,64,2560]{2,1,0:T(8,128)(2,1)S(1)} copy-done((bf16[32,64,2560]{2,1,0:T(8,128)(2,1)S(1)}, bf16[32,64,2560]{2,1,0:T(8,128)(2,1)}, u32[]{:S(2)}) %copy-start) | copy-done | bytes 10485784
  7.2 0.0 copy-start.3
  7.2 0.7 copy-done.3
  7.9 0.0 copy-start.8
  7.9 0.0 copy-start.5
  7.9 0.0 copy-start.6
  7.9 0.0 copy-start.4
  7.9 10.0 %shard_map.109 = (bf16[2,64,2560]{2,1,0:T(8,128)(2,1)S(1)}, bf16[34,64,128]{2,1,0:T(8,128)(2,1)S(1)}, s32[8,8,128]{2,1,0:T(8,128)S(1)}, s32[3,3,8,128]{3,2,1,0:T(8,128)S(1)}) custom-call(bf16[32,64,2560]{2,1,0:T(8,128)(2,1)S(1)} %copy-done, s32[1,20]{1,0:T(1,128)S(1)} %copy-done.3), custom_call_target="tpu_custom_call" | custom-call | bytes 2000000 | tf_op jit(solution)/shard_map/pallas_call | solution.py:346
  17.9 0.0 copy-start.7
  17.9 0.8 slice_reduce_fusion.1
  18.7 0.7 and_select_fusion.3
  19.3 0.0 copy-done.8
  19.4 0.1 select_reduce_fusion.7
  19.5 0.1 reshape_squeeze.4
  19.6 0.1 slice_bitcast_fusion.3
  19.7 0.2 select_reduce_fusion.8
  19.9 0.2 select_reduce_fusion.1
  20.1 0.1 copy.77
  20.2 0.1 reshape.286.flags_ref
  20.3 0.0 copy-done.5
  20.3 0.2 copy.71
  20.5 0.0 copy-done.6
  20.5 0.1 broadcast_in_dim_tile.6.b1_ref
  20.6 0.0 copy-done.4
  20.6 0.3 reshape.282
  20.9 0.6 fusion.6
  21.6 0.0 copy-start.1
  21.6 0.0 copy-start.2
  21.6 0.8 copy.74
  22.4 0.8 copy.76
  23.2 0.8 copy.75
  24.0 0.0 copy-done.7
  24.0 0.1 broadcast_in_dim_tile.7.b2_ref
  24.1 0.2 maximum_maximum_fusion.1
  24.4 4.5 %maximum_maximum_fusion = bf16[3,3,256,256]{3,2,1,0:T(8,128)(2,1)S(1)} fusion(bf16[3,3,64,64]{3,2,1,0:T(8,128)(2,1)} %bitcast.68, bf16[3,3,64,64]{3,2,1,0:T(8,128)(2,1)} %bitcast.69, bf16[3,3,64,128]{3,2,1,0:T(8,128)(2,1)S(1)} %broadcast.312, bf16[3,3,64,64]{3,2,1,0:T(8,128)(2,1)} %bitcast.70, bf16[3,3,64,64]{3,2,1,0:T(8,128)(2,1)S(1)} %broadcast_in_dim.182), kind=kLoop, calls=%fused_computation.2 | loop fusion | flops 16515072 | bytes 1622016 | tf_op jit(solution)/shard_map/concatenate | solution.py:45
  28.9 0.0 copy-done.1
  28.9 0.0 copy-done.2
  28.9 15.2 %shard_map.111 = bf16[8,64,512]{2,1,0:T(8,128)(2,1)} custom-call(s32[1]{0:T(128)} %bitcast.26.n_ref, s32[4]{0:T(128)S(1)} %get-tuple-element.18.cols_ref, s32[4]{0:T(128)S(1)} %get-tuple-element.17.slots_ref, s32[36]{0:T(128)S(1)} %reshape.286.flags_ref, bf16[32,64,2560]{2,1,0:T(8,128)(2,1)} %next_ref.3, bf16[32,64,2560]{2,1,0:T(8,128)(2,1)} %next_ref.3, ...), custom_call_target="tpu_custom_call" | custom-call | flops 6400000000 | bytes 6400000 | tf_op jit(solution)/shard_map/pallas_call | solution.py:198
  44.2 4.1 %all-to-all-start.1 = ((bf16[8,64,512]{2,1,0:T(8,128)(2,1)}), bf16[8,64,512]{2,1,0:T(8,128)(2,1)}, u32[]{:S(2)}, u32[]{:S(2)}) async-start(bf16[8,64,512]{2,1,0:T(8,128)(2,1)} %shard_map.111), calls=%async_computation.1 | async-start | bytes 1048576 | tf_op jit(solution)/shard_map/all_to_all | solution.py:422
  48.9 0.2 select_reduce_fusion.3
  49.1 0.2 select_reduce_fusion
  49.3 0.1 copy.70
  49.4 0.1 reshape.279.flags_ref
  49.5 53.6 %shard_map.110 = bf16[16,64,512]{2,1,0:T(8,128)(2,1)} custom-call(s32[1]{0:T(128)} %bitcast.n_ref, s32[16]{0:T(128)S(1)} %get-tuple-element.16.cols_ref, s32[16]{0:T(128)S(1)} %get-tuple-element.15.slots_ref, s32[144]{0:T(256)S(1)} %reshape.279.flags_ref, bf16[32,64,2560]{2,1,0:T(8,128)(2,1)} %next_ref.3, bf16[32,64,2560]{2,1,0:T(8,128)(2,1)} %next_ref.3, ...), custom_call_target="tpu_custom_call" | custom-call | flops 25600000000 | bytes 25600000 | tf_op jit(solution)/shard_map/pallas_call | solution.py:198
  103.1 0.0 all-to-all-done.1
  103.1 5.0 %all-to-all-start = ((bf16[16,64,512]{2,1,0:T(8,128)(2,1)}), bf16[16,64,512]{2,1,0:T(8,128)(2,1)S(1)}, u32[]{:S(2)}, u32[]{:S(2)}) async-start(bf16[16,64,512]{2,1,0:T(8,128)(2,1)} %shard_map.110), calls=%async_computation | async-start | bytes 2097152 | tf_op jit(solution)/shard_map/all_to_all | solution.py:422
  108.1 0.1 select_reduce_fusion.6
  108.2 0.6 fusion.1
  108.8 0.6 multiply_add_fusion
  109.5 0.1 convert_reduce_fusion
  109.6 0.1 select_reduce_fusion.5
  109.7 0.7 fusion.3
  110.3 24.3 %all-to-all-done = bf16[16,64,512]{2,1,0:T(8,128)(2,1)S(1)} async-done(((bf16[16,64,512]{2,1,0:T(8,128)(2,1)}), bf16[16,64,512]{2,1,0:T(8,128)(2,1)S(1)}, u32[]{:S(2)}, u32[]{:S(2)}) %all-to-all-start) | async-done | bytes 1048608 | tf_op jit(solution)/shard_map/all_to_all | solution.py:422
  134.6 1.2 pad_maximum_fusion
  135.8 1.5 %gather_fusion = bf16[10,64,512]{2,1,0:T(8,128)(2,1)} fusion(bf16[24,64,512]{2,1,0:T(8,128)(2,1)S(1)} %bitcast.66, s32[1024]{0:T(1024)S(1)} %pad_clamp_fusion), kind=kCustom, calls=%fused_computation | custom fusion | bytes 1310760 | tf_op jit(solution)/shard_map/jit(_take)/gather | solution.py:433
  (14 shorter events, 0.2 us)
Async XLA Ops:
  3.2 4.0 %copy-start = (bf16[32,64,2560]{2,1,0:T(8,128)(2,1)S(1)}, bf16[32,64,2560]{2,1,0:T(8,128)(2,1)}, u32[]{:S(2)}) copy-start(bf16[32,64,2560]{2,1,0:T(8,128)(2,1)} %next_ref.3) | copy-start | bytes 31457284
  7.2 0.7 copy-start.3
  7.9 11.5 %copy-start.8 = (s32[1,8]{1,0:T(1,128)S(1)}, s32[1,8]{1,0:T(1,128)}, u32[]{:S(2)}) copy-start(s32[1,8]{1,0:T(1,128)} %param.13) | copy-start | bytes 100
  7.9 12.4 %copy-start.5 = (bf16[64,576]{1,0:T(8,128)(2,1)S(1)}, bf16[64,576]{1,0:T(8,128)(2,1)}, u32[]{:S(2)}) copy-start(bf16[64,576]{1,0:T(8,128)(2,1)} %param.14) | copy-start | bytes 221188
  7.9 12.6 %copy-start.6 = (f32[64]{0:T(128)S(1)}, f32[64]{0:T(128)}, u32[]{:S(2)}) copy-start(f32[64]{0:T(128)} %param.15) | copy-start | bytes 772
  7.9 12.7 %copy-start.4 = (bf16[64,1728]{1,0:T(8,128)(2,1)S(1)}, bf16[64,1728]{1,0:T(8,128)(2,1)}, u32[]{:S(2)}) copy-start(bf16[64,1728]{1,0:T(8,128)(2,1)} %param.16) | copy-start | bytes 663556
  17.9 6.1 %copy-start.7 = (f32[64]{0:T(128)S(1)}, f32[64]{0:T(128)}, u32[]{:S(2)}) copy-start(f32[64]{0:T(128)} %param.17) | copy-start | bytes 772
  21.6 7.3 %copy-start.1 = (bf16[2,256,512]{2,1,0:T(8,128)(2,1)S(1)}, bf16[2,256,512]{2,1,0:T(8,128)(2,1)}, u32[]{:S(2)}) copy-start(bf16[2,256,512]{2,1,0:T(8,128)(2,1)} %constant.81.clone.inter_ref) | copy-start | bytes 1572868
  21.6 7.3 %copy-start.2 = (bf16[160,256]{1,0:T(8,128)(2,1)S(1)}, bf16[160,256]{1,0:T(8,128)(2,1)}, u32[]{:S(2)}) copy-start(bf16[160,256]{1,0:T(8,128)(2,1)} %constant.80.clone.spread_ref) | copy-start | bytes 245764
  44.2 58.9 %all-to-all-start.1 = ((bf16[8,64,512]{2,1,0:T(8,128)(2,1)}), bf16[8,64,512]{2,1,0:T(8,128)(2,1)}, u32[]{:S(2)}, u32[]{:S(2)}) async-start(bf16[8,64,512]{2,1,0:T(8,128)(2,1)} %shard_map.111), calls=%async_computation.1 | async-start | bytes 1048576 | tf_op jit(solution)/shard_map/all_to_all | solution.py:422
  103.1 31.5 %all-to-all-start = ((bf16[16,64,512]{2,1,0:T(8,128)(2,1)}), bf16[16,64,512]{2,1,0:T(8,128)(2,1)S(1)}, u32[]{:S(2)}, u32[]{:S(2)}) async-start(bf16[16,64,512]{2,1,0:T(8,128)(2,1)} %shard_map.110), calls=%async_computation | async-start | bytes 2097152 | tf_op jit(solution)/shard_map/all_to_all | solution.py:422
